TPU v7x, 128 devices: a whole 4x4x4 slice. The times are simulated.
128 devices in a mesh: grp: 4 (over y_hi, core), chan: 16 (over z, x), tile: 2 (over y_lo).
Axes of the slice: x: 4, y: 4 (y_hi: 2, y_lo: 2; y = y_hi * 2 + y_lo), z: 4, core: 2. Of those that a mesh axis runs over, the one named last changes fastest.
Arguments:
- voltages: bfloat16 [1024, 512, 2, 1024], P(('grp', 'tile'), 'chan'), may hold values from -6 to 6
- taps: float32 [8, 1024], replicated, may hold values from -0.0625 to 0.0625
Outputs:
- vis_real: float32 [256, 36, 128, 128], P(('grp', 'chan', 'tile'))
- vis_imag: float32 [256, 36, 128, 128], P(('grp', 'chan', 'tile'))
All inputs are finite; a program needn't handle non-finite values.
Results may differ from a plain program's by a relative error of at most 0.004.
Values may be sent and summed in bfloat16 or wider, within the bound.
No kernel may reach another device: no remote copies, remote signals or barrier semaphores. Data moves between devices by JAX's collectives and lax.ppermute only.
A program may use at most 256 MiB of HBM per device.

v0:
```python
import math

import jax
import jax.numpy as jnp
from jax import lax
from jax.sharding import PartitionSpec as P

ANTENNA_COUNT = 1024
FRAME_SAMPLES = 1024
FILTER_TAPS = 8
ANTENNA_BLOCKS = 8
DEVICE_CHANNELS = 2
TILE_ANTENNAS = 128


def from_behind(block, axis, distance):
    devices = range(lax.axis_size(axis))
    route = [(i - distance, i) for i in devices if i - distance in devices]
    return lax.ppermute(block, axis, route)


def transform_table(length, window):
    sample = jnp.arange(length, dtype=jnp.int32)[:, None]
    channel = jnp.arange(window, dtype=jnp.int32)[None, :]
    angles = (sample * channel % length).astype(jnp.float32) * (2.0 * math.pi / length)
    cosine = jnp.cos(angles)
    sine_part = jnp.sin(angles)
    upper_half = jnp.concatenate([cosine, -sine_part], axis=1)
    bottom = jnp.concatenate([sine_part, cosine], axis=1)
    return jnp.concatenate([upper_half, bottom], axis=0)


def upper_tile_list(matrix):
    chans = matrix.shape[0]
    blocked = matrix.reshape(
        chans, ANTENNA_BLOCKS, TILE_ANTENNAS, ANTENNA_BLOCKS, TILE_ANTENNAS
    ).transpose(0, 1, 3, 2, 4)
    return jnp.concatenate(
        [blocked[:, row_block, row_block:] for row_block in range(ANTENNA_BLOCKS)], axis=1
    )


def apply_table(rows, fourier_transform):
    return jnp.dot(
        rows, fourier_transform, preferred_element_type=jnp.float32, precision=lax.Precision.HIGHEST
    )


def on_device(voltages, taps):
    local_antennas = voltages.shape[0]
    device_frames = voltages.shape[1]
    rim_frames = FILTER_TAPS - 1
    groups_total = lax.axis_size("grp")
    time_total = lax.axis_size("chan")
    tiles_total = lax.axis_size("tile")
    device_list = groups_total * time_total * tiles_total
    window = DEVICE_CHANNELS * device_list
    fourier_transform = transform_table(FRAME_SAMPLES, window)
    before = from_behind(voltages[:, device_frames - rim_frames :], "chan", 1)
    extended = jnp.concatenate([before, voltages], axis=1)
    running_total = jnp.zeros(voltages.shape, jnp.float32)
    for tap_index in range(FILTER_TAPS):
        offset_frame = rim_frames - tap_index
        frames = extended[:, offset_frame : offset_frame + device_frames].astype(jnp.float32)
        running_total = running_total + taps[tap_index][None, None, None, :] * frames
    frame_matrix = running_total.reshape(local_antennas * device_frames, 2 * FRAME_SAMPLES)
    spectra_stack = apply_table(frame_matrix, fourier_transform).astype(jnp.bfloat16)
    spectra_total = device_frames * time_total
    departing_data = spectra_stack.reshape(
        local_antennas, device_frames, 2, device_list, DEVICE_CHANNELS
    ).transpose(3, 4, 2, 1, 0)
    departing_data = departing_data.reshape(
        device_list, 1, DEVICE_CHANNELS, 2, device_frames, local_antennas
    )
    received_data = lax.all_to_all(
        departing_data, ("grp", "chan", "tile"), split_axis=0, concat_axis=1, tiled=True
    )
    received_data = received_data.reshape(
        groups_total, time_total, tiles_total, DEVICE_CHANNELS, 2, device_frames, local_antennas
    )
    channel_matrix = received_data.transpose(3, 0, 2, 6, 4, 1, 5).reshape(
        DEVICE_CHANNELS, ANTENNA_COUNT, 2 * spectra_total
    )
    inverse_count = 1.0 / spectra_total
    swapped = jnp.concatenate(
        [channel_matrix[:, :, spectra_total:], -channel_matrix[:, :, :spectra_total]], axis=2
    )
    stacked_rows = jnp.concatenate([channel_matrix, swapped], axis=1)
    cross_products = (
        jnp.einsum("cpk,cqk->cpq", stacked_rows, channel_matrix, preferred_element_type=jnp.float32)
        * inverse_count
    )
    real_tile_list = upper_tile_list(cross_products[:, :ANTENNA_COUNT])
    imaginary_tiles = upper_tile_list(cross_products[:, ANTENNA_COUNT:])
    return (real_tile_list, imaginary_tiles)


def solution(mesh):
    in_specs = (P(("grp", "tile"), "chan", None, None), P())
    out_specs = (
        P(("grp", "chan", "tile"), None, None, None),
        P(("grp", "chan", "tile"), None, None, None),
    )
    return jax.shard_map(
        on_device, mesh=mesh, in_specs=in_specs, out_specs=out_specs, check_vma=False
    )
```

profile of v0, /device:TPU:1, one launch (start us, length us, event | category | flops | bytes accessed | tf_op | source)
XLA Modules:
  0.0 502.1 jit_solution(11637409025324610688)
XLA Ops:
  0.6 0.0 copy-start.4
  0.6 4.6 slice.110
  5.2 4.6 collective-permute-start
  9.8 3.9 fusion.23
  13.6 4.1 fusion.21
  17.7 0.0 copy-done.4
  17.8 69.4 %collective-permute-done = bf16[128,7,2,1024]{3,2,1,0:T(2,128)(2,1)S(1)} collective-permute-done((bf16[128,7,2,1024]{3,2,1,0:T(2,128)(2,1)S(1)}, bf16[128,7,2,1024]{3,2,1,0:T(2,128)(2,1)S(1)}, u32[]{:S(2)}, u32[]{:S(2)}) %collective-permute-start) | collective-permute-done | bytes 3670048 | tf_op jit(solution)/shard_map/ppermute | solution.py:19
  87.2 0.0 slice-start
  87.2 4.4 constant_dynamic-update-slice_fusion.1
  91.6 0.0 slice-start.1
  91.6 0.0 slice-start.2
  91.6 0.0 slice-start.3
  91.6 25.9 %constant_dynamic-update-slice_fusion = bf16[128,39,2,1024]{3,2,1,0:T(2,128)(2,1)} fusion(bf16[128,39,2,1024]{3,2,1,0:T(2,128)(2,1)} %constant_dynamic-update-slice_fusion.1, bf16[128,32,2,1024]{3,2,1,0:T(2,128)(2,1)} %param.2), kind=kLoop, calls=%fused_computation.64 | loop fusion | bytes 33554432 | tf_op jit(solution)/shard_map/concatenate | solution.py:60
  117.5 0.0 slice-done
  117.5 0.0 slice-done.1
  117.5 0.0 slice-done.2
  117.5 0.0 slice-done.3
  117.6 118.2 %multiply_add_fusion = f32[128,32,2,1024]{3,2,1,0:T(2,128)} fusion(bf16[128,32,2,1024]{3,2,1,0:T(2,128)(2,1)S(1)} %bitcast.91, bf16[128,39,2,1024]{3,2,1,0:T(2,128)(2,1)} %constant_dynamic-update-slice_fusion, f32[1024]{0:T(1024)S(1)} %bitcast.122, f32[1024]{0:T(1024)S(1)} %bitcast.123, f32[1024]{0:T(1024)S(1)} %bitcast.117, f32[1024]{0:T(1024)S(1)} %bitcast.118, ...), kind=kLoop, calls=%fused_computation | loop fusion | flops 192937984 | bytes 167804928 | tf_op jit(solution)/shard_map/add | solution.py:65
  235.7 30.0 %copy.67 = f32[512,8,2,1024]{3,1,2,0:T(8,128)} copy(f32[512,8,2,1024]{3,2,1,0:T(2,128)} %bitcast.89) | data formatting | bytes 67108864
  265.7 57.0 %convolution_convert_fusion = bf16[4096,512]{1,0:T(8,128)(2,1)} fusion(f32[4096,2048]{1,0:T(8,128)} %bitcast.93, f32[1024,256]{1,0:T(8,128)S(1)} %get-tuple-element.15, f32[1024,256]{1,0:T(8,128)S(1)} %get-tuple-element.14, f32[1024,256]{1,0:T(8,128)S(1)} %fusion.23), kind=kOutput, calls=%fused_computation.10 | convolution fusion | flops 51544850432 | bytes 40894464 | tf_op jit(solution)/shard_map/dot_general | solution.py:44
  322.7 6.7 %copy.43 = bf16[4096,512]{0,1:T(8,128)(2,1)} copy(bf16[4096,512]{1,0:T(8,128)(2,1)} %convolution_convert_fusion) | data formatting | bytes 8388608 | tf_op jit(solution)/shard_map/convert_element_type | solution.py:67
  329.4 17.3 %reshape.38 = bf16[128,32,2,128,2]{1,0,4,3,2:T(8,128)(2,1)} reshape(bf16[4096,512]{0,1:T(8,128)(2,1)} %copy.43) | data formatting | bytes 8388608 | tf_op jit(solution)/shard_map/reshape | solution.py:69
  346.7 14.2 %copy.44 = bf16[128,1,2,2,32,128]{5,4,3,2,1,0:T(8,128)(2,1)} copy(bf16[128,1,2,2,32,128]{4,5,2,0,3,1:T(8,128)(2,1)} %bitcast.92) | data formatting | bytes 8388608 | tf_op jit(solution)/shard_map/reshape | solution.py:72
  360.9 65.1 %all_to_all.4 = bf16[128,1,2,2,32,128]{5,4,3,2,1,0:T(8,128)(2,1)S(1)} all-to-all(bf16[128,1,2,2,32,128]{5,4,3,2,1,0:T(8,128)(2,1)} %copy.44), channel_id=1, replica_groups=mesh['grp'=4,'chan'=16,'tile'=2] {'grp','chan','tile'}, dimensions={0} | all-to-all | bytes 8388608 | tf_op jit(solution)/shard_map/all_to_all | solution.py:75
  426.1 6.3 %copy.89 = bf16[4,16,2,2,2,32,128]{6,2,0,5,1,4,3:T(2,128)(2,1)} copy(bf16[4,16,2,2,2,32,128]{6,5,4,3,2,1,0:T(8,128)(2,1)S(1)} %bitcast.114) | data formatting | bytes 8388608 | tf_op jit(solution)/shard_map/reshape | solution.py:78
  432.4 7.7 %reshape.41 = bf16[2,1024,1024]{1,2,0:T(8,128)(2,1)} reshape(bf16[2,4,2,128,2,16,32]{3,2,1,6,5,4,0:T(2,128)(2,1)} %bitcast.115) | data formatting | bytes 8388608 | tf_op jit(solution)/shard_map/reshape | solution.py:81
  440.1 6.2 %copy.48 = bf16[2,1024,1024]{2,1,0:T(8,128)(2,1)} copy(bf16[2,1024,1024]{1,2,0:T(8,128)(2,1)} %reshape.41) | data formatting | bytes 8388608 | tf_op jit(solution)/shard_map/reshape | solution.py:81
  446.3 0.0 copy-start
  446.3 0.0 copy-start.1
  446.3 4.8 fusion.29
  451.0 0.0 copy-done
  451.1 1.5 copy-done.1
  452.5 14.0 %broadcast_multiply_fusion = f32[2,2048,1024]{2,1,0:T(8,128)} fusion(bf16[2,1024,1024]{1,2,0:T(8,128)(2,1)S(1)} %copy-done, bf16[2,1024,512]{2,1,0:T(8,128)(2,1)} %get-tuple-element.5, bf16[2,1024,512]{2,1,0:T(8,128)(2,1)} %get-tuple-element.4, bf16[2,1024,1024]{2,1,0:T(8,128)(2,1)S(1)} %copy-done.1), kind=kOutput, calls=%fused_computation.9 | convolution fusion | flops 8619294720 | bytes 29360128 | tf_op jit(solution)/shard_map/cpk,cqk->cpq/dot_general | solution.py:90
  466.5 9.5 %fusion.28 = (f32[2,1024,1024]{2,1,0:T(8,128)}, f32[2,1024,1024]{2,1,0:T(8,128)S(1)}) fusion(f32[2,2048,1024]{2,1,0:T(8,128)} %broadcast_multiply_fusion), kind=kLoop, calls=%fused_computation.68 | loop fusion | bytes 33554432 | tf_op jit(solution)/shard_map/slice | solution.py:94
  476.0 5.5 %copy.69 = f32[256,8,8,128]{3,2,1,0:T(8,128)S(1)} copy(f32[256,8,8,128]{3,1,2,0:T(8,128)} %bitcast.97) | data formatting | bytes 16777216
  481.5 4.7 copy.87
  486.2 1.3 copy_dynamic-update-slice_fusion
  487.5 1.2 copy_dynamic-update-slice_fusion.2
  488.8 1.2 copy_dynamic-update-slice_fusion.4
  490.0 1.1 copy_dynamic-update-slice_fusion.6
  491.1 1.1 copy_dynamic-update-slice_fusion.8
  492.2 1.0 copy_dynamic-update-slice_fusion.10
  493.2 1.0 copy_dynamic-update-slice_fusion.12
  494.2 0.9 fusion.24
  495.1 0.0 copy-start.2
  495.1 2.2 copy.68
  497.3 0.5 copy-done.2
  497.8 1.5 copy.88
  499.3 0.1 copy_dynamic-update-slice_fusion.1
  499.4 0.1 copy_dynamic-update-slice_fusion.3
  499.5 0.1 copy_dynamic-update-slice_fusion.5
  499.7 0.0 copy-start.3
  499.7 2.2 copy-done.3
  (7 shorter events, 0.2 us)
Async XLA Ops:
  0.6 17.1 %copy-start.4 = (f32[8,1024]{1,0:T(8,128)S(1)}, f32[8,1024]{1,0:T(8,128)}, u32[]{:S(2)}) copy-start(f32[8,1024]{1,0:T(8,128)} %param.3) | copy-start | bytes 98308
  5.2 81.9 %collective-permute-start = (bf16[128,7,2,1024]{3,2,1,0:T(2,128)(2,1)S(1)}, bf16[128,7,2,1024]{3,2,1,0:T(2,128)(2,1)S(1)}, u32[]{:S(2)}, u32[]{:S(2)}) collective-permute-start(bf16[128,7,2,1024]{3,2,1,0:T(2,128)(2,1)S(1)} %slice.110), channel_id=1, source_target_pairs={{0,2},{2,4},{4,6},{6,8},{8,10},{10,12},{12,14},{14,16},{16,18},{18... | collective-permute-start | bytes 11010056 | tf_op jit(solution)/shard_map/ppermute | solution.py:19
  87.2 30.4 %slice-start = ((s8[16777216]{0:T(1024)(128)(4,1)}), s8[4194304]{0:T(1024)(128)(4,1)S(1)}, s32[]{:S(2)}) async-start(s8[16777216]{0:T(1024)(128)(4,1)} %bitcast.90), calls=%async_computation.1 | async-start | bytes 8388608
  91.6 25.9 %slice-start.1 = ((s8[16777216]{0:T(1024)(128)(4,1)}), s8[4194304]{0:T(1024)(128)(4,1)S(1)}, s32[]{:S(2)}) async-start(s8[16777216]{0:T(1024)(128)(4,1)} %bitcast.90), calls=%async_computation.2 | async-start | bytes 8388608
  91.6 25.9 %slice-start.2 = ((s8[16777216]{0:T(1024)(128)(4,1)}), s8[4194304]{0:T(1024)(128)(4,1)S(1)}, s32[]{:S(2)}) async-start(s8[16777216]{0:T(1024)(128)(4,1)} %bitcast.90), calls=%async_computation.3 | async-start | bytes 8388608
  91.6 25.9 %slice-start.3 = ((s8[16777216]{0:T(1024)(128)(4,1)}), s8[4194304]{0:T(1024)(128)(4,1)S(1)}, s32[]{:S(2)}) async-start(s8[16777216]{0:T(1024)(128)(4,1)} %bitcast.90), calls=%async_computation.4 | async-start | bytes 8388608
  446.3 4.8 copy-start
  446.3 6.2 %copy-start.1 = (bf16[2,1024,1024]{2,1,0:T(8,128)(2,1)S(1)}, bf16[2,1024,1024]{2,1,0:T(8,128)(2,1)}, u32[]{:S(2)}) copy-start(bf16[2,1024,1024]{2,1,0:T(8,128)(2,1)} %copy.48) | copy-start | bytes 12582916
  495.1 2.7 copy-start.2
  499.7 2.2 copy-start.3
where the time goes:
time: 503 us; the launch traced here: 502 us
  local copies, waits for them, and re-layouts  160 us (32%)
  other arithmetic  131 us (26%)
  matrix products  71 us (14%)
  waiting for transfers between devices  69.4 us (14%)
  blocking collectives  65.1 us (13%)
    add x1, other arithmetic, on_device(): running_total + taps[tap_index][None, None, None, :] * frames  118 us
    ppermute x1, waiting for transfers between devices, from_behind(): return lax.ppermute(block, axis, route)  69.4 us
    all_to_all x1, blocking collectives, on_device(): lax.all_to_all(departing_data, ('grp', 'chan', 'tile'), split_axis=0, con...  65.1 us
    dot_general x1, matrix products, apply_table(): jnp.dot(rows, fourier_transform, preferred_element_type=jnp.float32, prec...  57 us
    unnamed x36, local copies, waits for them, and re-layouts  54.5 us
    concatenate x1, local copies, waits for them, and re-layouts, on_device(): extended = jnp.concatenate([before, voltages], axis=1)  25.9 us
    reshape x1, local copies, waits for them, and re-layouts, on_device(): spectra_stack.reshape(local_antennas, device_frames, 2, device_list, DEVI...  17.3 us
    reshape x1, local copies, waits for them, and re-layouts, on_device(): departing_data.reshape(device_list, 1, DEVICE_CHANNELS, 2, device_frames,...  14.2 us
  transfers between devices with their start and end apart: 1, of which 1 were waited for; matrix products, arithmetic and copies ran while one was open for 2% of the time, Pallas kernels for 0%

commit v1 on v0

v1 whole, which is shorter than its diff:
```python
import functools

import jax
import jax.numpy as jnp
import ml_dtypes
import numpy as np
from jax import lax
from jax.experimental import pallas as pl
from jax.experimental.pallas import tpu as pltpu
from jax.sharding import PartitionSpec as P

ANTENNA_COUNT = 1024
FRAME_SAMPLES = 1024
FILTER_TAPS = 8
ANTENNA_BLOCKS = 8
SPECTRA_COUNT = 512
DEVICE_CHANNELS = 2
TILE_ANTENNAS = 128
DEVICES = 128
FRAMES = 32
CHUNK = 8
OUT_FRAMES = FRAMES + CHUNK
HALF = FRAME_SAMPLES // 2
AXES = ("grp", "chan", "tile")


def transform_tables():
    sample = np.arange(HALF)
    parts = []
    for odd in range(2):
        channel = 2 * np.arange(DEVICES) + odd
        angle = 2.0 * np.pi * ((sample[:, None] * channel[None, :]) % FRAME_SAMPLES) / FRAME_SAMPLES
        cosine, sine = np.cos(angle), np.sin(angle)
        from_real = np.concatenate([cosine, -sine], axis=1)
        from_imag = np.concatenate([sine, cosine], axis=1)
        both = np.stack([from_real.reshape(4, 128, 256), from_imag.reshape(4, 128, 256)], axis=1)
        parts.append(both.reshape(FRAME_SAMPLES, 256))
    table = np.stack(parts).astype(np.float32)
    high = table.astype(ml_dtypes.bfloat16)
    low = (table - high.astype(np.float32)).astype(ml_dtypes.bfloat16)
    return high, low


def filterbank_kernel(x_hbm, taps_ref, high_ref, low_ref, out_ref, x_v, plus, minus, spectra, sems):
    z_refs = (plus, minus)
    chunks = FRAMES // CHUNK
    copies = [
        pltpu.make_async_copy(
            x_hbm.at[:, pl.ds(CHUNK * i, CHUNK)], x_v.at[:, pl.ds(CHUNK * i, CHUNK)], sems.at[i]
        )
        for i in range(chunks)
    ]
    for copy in copies:
        copy.start()
    for i in range(chunks + 1):
        if i < chunks:
            copies[i].wait()

        def filter_antenna(a, _):
            frames = {
                s: x_v[a, s].astype(jnp.float32)
                for s in range(CHUNK * i - FILTER_TAPS + 1, CHUNK * (i + 1))
                if 0 <= s < FRAMES
            }
            rows = pl.ds(pl.multiple_of(a * 8, 8), 8)
            for q in range(CHUNK):
                total = jnp.zeros((16, 128), jnp.float32)
                for k in range(FILTER_TAPS):
                    s = CHUNK * i + q - k
                    if s in frames:
                        total = total + taps_ref[k] * frames[s]
                plus[q, rows, :] = total[:8] + total[8:]
                minus[q, rows, :] = total[:8] - total[8:]
            return 0

        lax.fori_loop(0, TILE_ANTENNAS, filter_antenna, 0, unroll=2)
        for odd in range(2):

            def transform(q, _):
                highs, lows = [], []
                for row in range(8):
                    z = jnp.concatenate(
                        [z_refs[odd][2 * q + e, pl.ds(row, TILE_ANTENNAS, stride=8), :] for e in range(2)],
                        axis=0,
                    )
                    high = z.astype(jnp.bfloat16)
                    highs.append(high)
                    lows.append((z - high.astype(jnp.float32)).astype(jnp.bfloat16))
                high = jnp.concatenate(highs, axis=1)
                low = jnp.concatenate(lows, axis=1)
                dot = functools.partial(jnp.dot, preferred_element_type=jnp.float32)
                found = (
                    dot(high, high_ref[odd]) + dot(low, high_ref[odd]) + dot(high, low_ref[odd])
                ).T
                for e in range(2):
                    spectra[odd, pl.ds(2 * q + e, 256, stride=CHUNK), :] = found[:, 128 * e : 128 * e + 128]
                return 0

            lax.fori_loop(0, CHUNK // 2, transform, 0)
            for part in range(2):
                rows = spectra[odd, 1024 * part : 1024 * part + 1024, :].reshape(DEVICES, CHUNK, 128)
                out_ref[:, odd, part, CHUNK * i : CHUNK * (i + 1), :] = rows.astype(jnp.bfloat16)


def filterbank(voltages, taps):
    frames = voltages.reshape(TILE_ANTENNAS, FRAMES, 2, 8, 128).transpose(0, 1, 3, 2, 4)
    frames = frames.reshape(TILE_ANTENNAS, FRAMES, 16, 128)
    taps_rows = jnp.broadcast_to(taps.reshape(8, 8, 1, 128), (8, 8, 2, 128)).reshape(8, 16, 128)
    high, low = transform_tables()
    vmem = pl.BlockSpec(memory_space=pltpu.VMEM)
    return pl.pallas_call(
        filterbank_kernel,
        out_shape=jax.ShapeDtypeStruct((DEVICES, 2, 2, OUT_FRAMES, 128), jnp.bfloat16),
        in_specs=[pl.BlockSpec(memory_space=pl.ANY), vmem, vmem, vmem],
        out_specs=vmem,
        scratch_shapes=[
            pltpu.VMEM((TILE_ANTENNAS, FRAMES, 16, 128), jnp.bfloat16),
            pltpu.VMEM((CHUNK, 1024, 128), jnp.float32),
            pltpu.VMEM((CHUNK, 1024, 128), jnp.float32),
            pltpu.VMEM((2, 256 * CHUNK, 128), jnp.float32),
            pltpu.SemaphoreType.DMA((4,)),
        ],
        compiler_params=pltpu.CompilerParams(vmem_limit_bytes=56 * 2**20),
    )(frames, taps_rows, jnp.asarray(high), jnp.asarray(low))


def correlate_kernel(in_ref, real_ref, imag_ref, y, yt):
    for b in range(ANTENNA_BLOCKS):
        grp, tile = b // 2, b % 2
        for part in range(2):

            def join(t, _):
                src = (grp * 16 + t) * 2 + tile
                before = jnp.maximum(src - 2, 0)
                tail = in_ref[before, 0, part, FRAMES:OUT_FRAMES, :].astype(jnp.float32)
                tail = jnp.where(t > 0, tail, 0.0)
                own = in_ref[src, 0, part, 0:FRAMES, :]
                head = (own[:CHUNK].astype(jnp.float32) + tail).astype(jnp.bfloat16)
                rows = pl.ds(pl.multiple_of(part * 512 + t * FRAMES, FRAMES), FRAMES)
                y[rows, 128 * b : 128 * b + 128] = jnp.concatenate([head, own[CHUNK:]], axis=0)
                return 0

            lax.fori_loop(0, 16, join, 0, unroll=4)
        yt[128 * b : 128 * b + 128, :] = y[:, 128 * b : 128 * b + 128].T
    dot = functools.partial(jnp.dot, preferred_element_type=jnp.float32)
    scale = 1.0 / SPECTRA_COUNT

    def first(i):
        return ANTENNA_BLOCKS * i - i * (i - 1) // 2

    for pair in range(ANTENNA_BLOCKS // 2):
        rows = yt[256 * pair : 256 * pair + 256, :]
        for other in range(pair, ANTENNA_BLOCKS // 2):
            columns = slice(256 * other, 256 * other + 256)
            real = dot(rows, y[:, columns]) * scale
            imag = (dot(rows[:, 512:], y[:512, columns]) - dot(rows[:, :512], y[512:, columns])) * scale
            for a in range(2):
                for b in range(2):
                    i, j = 2 * pair + a, 2 * other + b
                    if i <= j:
                        p = first(i) + j - i
                        real_ref[0, p] = real[128 * a : 128 * a + 128, 128 * b : 128 * b + 128]
                        imag_ref[0, p] = imag[128 * a : 128 * a + 128, 128 * b : 128 * b + 128]


def correlate(received):
    pairs = ANTENNA_BLOCKS * (ANTENNA_BLOCKS + 1) // 2
    out = jax.ShapeDtypeStruct((DEVICE_CHANNELS, pairs, 128, 128), jnp.float32)
    out_spec = pl.BlockSpec((1, pairs, 128, 128), lambda c: (c, 0, 0, 0))
    return pl.pallas_call(
        correlate_kernel,
        grid=(DEVICE_CHANNELS,),
        out_shape=(out, out),
        in_specs=[pl.BlockSpec((DEVICES, 1, 2, OUT_FRAMES, 128), lambda c: (0, c, 0, 0, 0))],
        out_specs=(out_spec, out_spec),
        scratch_shapes=[
            pltpu.VMEM((1024, ANTENNA_COUNT), jnp.bfloat16),
            pltpu.VMEM((ANTENNA_COUNT, 1024), jnp.bfloat16),
        ],
        compiler_params=pltpu.CompilerParams(vmem_limit_bytes=56 * 2**20),
    )(received)


def on_device(voltages, taps):
    departing = filterbank(voltages, taps)
    received = lax.all_to_all(departing, AXES, split_axis=0, concat_axis=0, tiled=True)
    return correlate(received)


def solution(mesh):
    in_specs = (P(("grp", "tile"), "chan", None, None), P())
    out_specs = (P(AXES, None, None, None), P(AXES, None, None, None))
    return jax.shard_map(
        on_device, mesh=mesh, in_specs=in_specs, out_specs=out_specs, check_vma=False
    )
```

time: 503 us -> 149 us (0.30)
  local copies, waits for them, and re-layouts: 160 us -> 1.42 us
  other arithmetic: 131 us -> 0 us
  matrix products: 71 us -> 0 us
  Pallas kernels: 0 us -> 70.5 us
  waiting for transfers between devices: 69.4 us -> 0 us
  blocking collectives: 65.1 us -> 76.1 us
    add x1 -> x0, other arithmetic: 118 us -> none  [on_device(): running_total + taps[tap_index][None, None, None, :] * frames]
    dot_general x2 -> x0, matrix products: 71 us -> none  [the longest x1 57 us: apply_table(): jnp.dot(rows, fourier_transform, preferred_element_type=jnp.float32, prec...]
    pallas_call x0 -> x2, Pallas kernels: none -> 70.5 us  [the longest x1 56.1 us: filterbank(): pl.pallas_call(filterbank_kernel, out_shape=jax.ShapeDtypeStruct((DEVICES...]
    ppermute x1 -> x0, waiting for transfers between devices: 69.4 us -> none  [from_behind(): return lax.ppermute(block, axis, route)]
    reshape x7 -> x0, local copies, waits for them, and re-layouts: 57.9 us -> none  [the longest x1 17.3 us: on_device(): spectra_stack.reshape(local_antennas, device_frames, 2, device_list, DEVI...]
    unnamed x36 -> x0, local copies, waits for them, and re-layouts: 54.5 us -> none
    concatenate x3 -> x0, local copies, waits for them, and re-layouts: 26.8 us -> none  [the longest x1 25.9 us: on_device(): extended = jnp.concatenate([before, voltages], axis=1)]
    slice x3 -> x0, local copies, waits for them, and re-layouts: 14.1 us -> none  [the longest x1 9.5 us: on_device(): imaginary_tiles = upper_tile_list(cross_products[:, ANTENNA_COUNT:])]
  transfers between devices with their start and end apart: 1 -> 0, of which waited for: 1 -> 0; matrix products, arithmetic and copies ran while one was open for 2% -> 0% of each run, Pallas kernels for 0% -> 0%
where the time goes in v1:
time: 149 us
  blocking collectives  76.1 us (51%)
  Pallas kernels  70.5 us (47%)
    all_to_all x1, blocking collectives, on_device(): lax.all_to_all(departing, AXES, split_axis=0, concat_axis=0, tiled=True)  76.1 us
    pallas_call x1, Pallas kernels, filterbank(): pl.pallas_call(filterbank_kernel, out_shape=jax.ShapeDtypeStruct((DEVICES...  56.1 us
    pallas_call x1, Pallas kernels, correlate(): pl.pallas_call(correlate_kernel, grid=(DEVICE_CHANNELS,), out_shape=(out,...  14.4 us

profile of v1, /device:TPU:1, one launch (start us, length us, event | category | flops | bytes accessed | tf_op | source)
XLA Modules:
  0.0 148.7 jit_solution(18138159881502966874)
XLA Ops:
  0.6 0.8 copy.7
  1.4 0.7 broadcast_in_dim.8
  2.0 56.1 %shard_map.59 = bf16[128,2,2,40,128]{4,3,2,1,0:T(8,128)(2,1)} custom-call(bf16[128,32,16,128]{3,2,1,0:T(8,128)(2,1)} %bitcast.7, f32[8,16,128]{2,1,0:T(8,128)} %bitcast.8, bf16[2,1024,256]{2,1,0:T(8,128)(2,1)} %constant.4.clone.high_ref, bf16[2,1024,256]{2,1,0:T(8,128)(2,1)} %constant.5.clone.low_ref), custom_call_target="tpu_custom_call" | custom-call | tf_op jit(solution)/shard_map/pallas_call | solution.py:111
  58.2 76.1 %all_to_all.5.in_ref = bf16[128,2,2,40,128]{4,3,2,1,0:T(8,128)(2,1)} all-to-all(bf16[128,2,2,40,128]{4,3,2,1,0:T(8,128)(2,1)} %shard_map.59), channel_id=1, replica_groups=mesh['grp'=4,'chan'=16,'tile'=2] {'grp','chan','tile'}, dimensions={0} | all-to-all | bytes 10485760 | tf_op jit(solution)/shard_map/all_to_all | solution.py:186
  134.3 14.4 %shard_map.60 = (f32[2,36,128,128]{3,2,1,0:T(8,128)}, f32[2,36,128,128]{3,2,1,0:T(8,128)}) custom-call(bf16[128,2,2,40,128]{4,3,2,1,0:T(8,128)(2,1)} %all_to_all.5.in_ref), custom_call_target="tpu_custom_call" | custom-call | tf_op jit(solution)/shard_map/pallas_call | solution.py:170

commit v2 on v1

v2 whole, which is shorter than its diff:
```python
import functools

import jax
import jax.numpy as jnp
import ml_dtypes
import numpy as np
from jax import lax
from jax.experimental import pallas as pl
from jax.experimental.pallas import tpu as pltpu
from jax.sharding import PartitionSpec as P

ANTENNA_COUNT = 1024
FRAME_SAMPLES = 1024
FILTER_TAPS = 8
ANTENNA_BLOCKS = 8
SPECTRA_COUNT = 512
DEVICE_CHANNELS = 2
TILE_ANTENNAS = 128
DEVICES = 128
FRAMES = 32
UNIT = 8
PIECE = 4
TIME_BLOCKS = 16
PAIRS = ANTENNA_BLOCKS * (ANTENNA_BLOCKS + 1) // 2
HALF = FRAME_SAMPLES // 2
AXES = ("grp", "chan", "tile")

EARLY_UNITS = (0, 32, 8)
LATE_UNITS = (16, 24)
KEPT = 16
DEPTH = KEPT * TIME_BLOCKS


def transform_tables():
    sample = np.arange(HALF)
    parts = []
    for odd in range(2):
        channel = 2 * np.arange(DEVICES) + odd
        angle = 2.0 * np.pi * ((sample[:, None] * channel[None, :]) % FRAME_SAMPLES) / FRAME_SAMPLES
        cosine, sine = np.cos(angle), np.sin(angle)
        from_real = np.concatenate([cosine, -sine], axis=1)
        from_imag = np.concatenate([sine, cosine], axis=1)
        both = np.stack([from_real.reshape(4, 128, 256), from_imag.reshape(4, 128, 256)], axis=1)
        parts.append(both.reshape(FRAME_SAMPLES, 256))
    table = np.stack(parts).astype(np.float32)
    high = table.astype(ml_dtypes.bfloat16)
    low = (table - high.astype(np.float32)).astype(ml_dtypes.bfloat16)
    return high, low


def filterbank_kernel(units, order, x_hbm, taps_ref, high_hbm, low_hbm, out_hbm, *scratch):
    x_v, taps_rows, high_ref, low_ref, z, spectra, out_v, x_sems, table_sems, out_sems = scratch
    slot = {piece: i for i, piece in enumerate(order)}
    copies = [
        pltpu.make_async_copy(
            x_hbm.at[:, pl.ds(PIECE * piece, PIECE)], x_v.at[:, pl.ds(PIECE * i, PIECE)], x_sems.at[i]
        )
        for i, piece in enumerate(order)
    ]
    tables = [
        pltpu.make_async_copy(high_hbm, high_ref, table_sems.at[0]),
        pltpu.make_async_copy(low_hbm, low_ref, table_sems.at[1]),
    ]
    for copy in copies[:2] + tables + copies[2:]:
        copy.start()
    for k in range(FILTER_TAPS):
        for j in range(8):
            row = taps_ref[k : k + 1, 128 * j : 128 * j + 128]
            taps_rows[k, 2 * j : 2 * j + 2, :] = jnp.broadcast_to(row, (2, 128))

    def inputs(start):
        return [s for s in range(start - FILTER_TAPS + 1, start + UNIT) if 0 <= s < FRAMES]

    def filter_antenna(start, a):
        frames = {
            s: x_v[a, slot[s // PIECE] * PIECE + s % PIECE].astype(jnp.float32) for s in inputs(start)
        }
        rows = pl.ds(pl.multiple_of(a * 8, 8), 8)
        for q in range(UNIT):
            total = None
            for k in range(FILTER_TAPS):
                s = start + q - k
                if s in frames:
                    term = taps_rows[k] * frames[s]
                    total = term if total is None else total + term
            if total is None:
                total = jnp.zeros((16, 128), jnp.float32)
            z[0, q, rows, :] = total[:8] + total[8:]
            z[1, q, rows, :] = total[:8] - total[8:]

    def transform(u, odd):
        highs, lows = [], []
        for row in range(8):
            piece = jnp.concatenate(
                [z[odd, e, pl.ds(row, TILE_ANTENNAS, stride=8), :] for e in range(UNIT)], axis=0
            )
            high = piece.astype(jnp.bfloat16)
            highs.append(high)
            lows.append((piece - high.astype(jnp.float32)).astype(jnp.bfloat16))
        high = jnp.concatenate(highs, axis=1)
        low = jnp.concatenate(lows, axis=1)
        count = UNIT * TILE_ANTENNAS
        dot = functools.partial(jnp.dot, preferred_element_type=jnp.float32)
        both = dot(jnp.concatenate([high, low], axis=0), high_ref[odd])
        found = (both[:count] + both[count:] + dot(high, low_ref[odd])).T
        for e in range(UNIT):
            spectra[pl.ds(e, 256, stride=UNIT), :] = found[:, 128 * e : 128 * e + 128]
        for part in range(2):
            rows = spectra[128 * UNIT * part : 128 * UNIT * (part + 1), :]
            out_v[:, odd, part, UNIT * u : UNIT * (u + 1), :] = rows.reshape(DEVICES, UNIT, 128).astype(
                jnp.bfloat16
            )

    leaving = [
        pltpu.make_async_copy(out_v.at[:, odd], out_hbm.at[:, odd], out_sems.at[odd]) for odd in range(2)
    ]
    waited = 0
    for u, start in enumerate(units):
        last = max(slot[s // PIECE] for s in inputs(start))
        while waited <= last:
            copies[waited].wait()
            waited += 1

        def filter_step(a, _, start=start):
            filter_antenna(start, a)
            return 0

        lax.fori_loop(0, TILE_ANTENNAS, filter_step, 0, unroll=2)
        if u == 0:
            for copy in tables:
                copy.wait()
        if u + 1 < len(units):

            def transform_step(odd, _, u=u):
                transform(u, odd)
                return 0

            lax.fori_loop(0, 2, transform_step, 0)
        else:
            for odd in range(2):
                transform(u, odd)
                leaving[odd].start()
    for copy in leaving:
        copy.wait()


def filterbank(frames, taps, high, low, units):
    order = []
    for start in units:
        for s in range(start - FILTER_TAPS + 1, start + UNIT):
            if 0 <= s < FRAMES and s // PIECE not in order:
                order.append(s // PIECE)
    span = UNIT * len(units)
    anywhere = pl.BlockSpec(memory_space=pl.ANY)
    shape = (DEVICES, 2, 2, span, 128)
    table = pltpu.VMEM((2, FRAME_SAMPLES, 256), jnp.bfloat16)
    return pl.pallas_call(
        functools.partial(filterbank_kernel, units, tuple(order)),
        out_shape=jax.ShapeDtypeStruct(shape, jnp.bfloat16),
        in_specs=[anywhere, pl.BlockSpec(memory_space=pltpu.VMEM), anywhere, anywhere],
        out_specs=anywhere,
        scratch_shapes=[
            pltpu.VMEM((TILE_ANTENNAS, PIECE * len(order), 16, 128), jnp.bfloat16),
            pltpu.VMEM((FILTER_TAPS, 16, 128), jnp.float32),
            table,
            table,
            pltpu.VMEM((2, UNIT, 1024, 128), jnp.float32),
            pltpu.VMEM((256 * UNIT, 128), jnp.float32),
            pltpu.VMEM(shape, jnp.bfloat16),
            pltpu.SemaphoreType.DMA((len(order),)),
            pltpu.SemaphoreType.DMA((2,)),
            pltpu.SemaphoreType.DMA((2,)),
        ],
        compiler_params=pltpu.CompilerParams(vmem_limit_bytes=60 * 2**20),
        cost_estimate=pl.CostEstimate(flops=30 * 10**9, bytes_accessed=20 * 2**20, transcendentals=0),
    )(frames, taps, high, low)


def store_left(left, ch, b, block):
    rows = pl.ds(128 * b, 128)
    turned = block.T
    left[ch, 0, rows, :] = turned
    left[ch, 1, rows, 0:DEPTH] = turned[:, DEPTH:]
    left[ch, 1, rows, DEPTH:] = -turned[:, :DEPTH]


def join_kernel(in_ref, y, left):
    def step(ch, _):
        for b in range(ANTENNA_BLOCKS):
            sources, tile = pl.ds((b // 2) * TIME_BLOCKS, TIME_BLOCKS), b % 2
            blocks = []
            for part in range(2):
                early = in_ref[sources, tile, ch, part, 0:8, :].astype(jnp.float32)
                tail = in_ref[sources, tile, ch, part, 8:16, :].astype(jnp.float32)
                rest = in_ref[sources, tile, ch, part, 16:24, :].astype(jnp.float32)
                none = jnp.zeros((1, 8, 128), jnp.float32)
                early = early + jnp.concatenate([none, tail[:-1]], axis=0)
                both = jnp.concatenate([early, rest], axis=1).astype(jnp.bfloat16)
                blocks.append(both.reshape(DEPTH, 128))
            block = jnp.concatenate(blocks, axis=0)
            y[ch, :, 128 * b : 128 * b + 128] = block
            store_left(left, ch, b, block)
        return 0

    lax.fori_loop(0, DEVICE_CHANNELS, step, 0)


def join(received):
    vmem = pl.BlockSpec(memory_space=pltpu.VMEM)
    return pl.pallas_call(
        join_kernel,
        out_shape=(
            jax.ShapeDtypeStruct((DEVICE_CHANNELS, 2 * DEPTH, ANTENNA_COUNT), jnp.bfloat16),
            jax.ShapeDtypeStruct((DEVICE_CHANNELS, 2, ANTENNA_COUNT, 2 * DEPTH), jnp.bfloat16),
        ),
        in_specs=[vmem],
        out_specs=(vmem, vmem),
        compiler_params=pltpu.CompilerParams(vmem_limit_bytes=60 * 2**20),
        cost_estimate=pl.CostEstimate(flops=5 * 10**9, bytes_accessed=12 * 2**20, transcendentals=0),
    )(received)


def correlate_kernel(in_hbm, y_hbm, left_hbm, real_hbm, imag_hbm, *scratch):
    in_ref, y, left, y_old, left_old, tiles, in_sems, old_sems, out_sems = scratch

    def arriving(ch):
        return pltpu.make_async_copy(in_hbm.at[:, :, ch], in_ref.at[:, :, ch], in_sems.at[ch])

    def arriving_old(ch):
        return (
            pltpu.make_async_copy(y_hbm.at[ch], y_old.at[ch], old_sems.at[ch, 0]),
            pltpu.make_async_copy(left_hbm.at[ch], left_old.at[ch], old_sems.at[ch, 1]),
        )

    for ch in range(DEVICE_CHANNELS):
        for copy in (arriving(ch), *arriving_old(ch)):
            copy.start()
    dot = functools.partial(jnp.dot, preferred_element_type=jnp.float32)

    def first(i):
        return ANTENNA_BLOCKS * i - i * (i - 1) // 2

    def prepare(ch):
        for b in range(ANTENNA_BLOCKS):
            sources, tile = pl.ds((b // 2) * TIME_BLOCKS, TIME_BLOCKS), b % 2
            block = jnp.concatenate(
                [in_ref[sources, tile, ch, part, :, :].reshape(DEPTH, 128) for part in range(2)], axis=0
            )
            y[ch, :, 128 * b : 128 * b + 128] = block
            store_left(left, ch, b, block)

    def leaving(ch, pair):
        some = pl.ds(first(2 * pair), first(2 * pair + 2) - first(2 * pair))
        return [
            pltpu.make_async_copy(tiles.at[ch, part, some], ref.at[ch, some], out_sems.at[ch, pair, part])
            for part, ref in enumerate((real_hbm, imag_hbm))
        ]

    def multiply(ch):
        for pair in range(ANTENNA_BLOCKS // 2):
            rows = pl.ds(256 * pair, 256)
            new = left[ch, :, rows, :].reshape(512, 2 * DEPTH)
            old = left_old[ch, :, rows, :].reshape(512, 2 * DEPTH)
            for other in range(pair, ANTENNA_BLOCKS // 2):
                columns = pl.ds(256 * other, 256)
                found = (dot(new, y[ch, :, columns]) + dot(old, y_old[ch, :, columns])) * (1.0 / SPECTRA_COUNT)
                for a in range(2):
                    for b in range(2):
                        i, j = 2 * pair + a, 2 * other + b
                        if i <= j:
                            for part in range(2):
                                top = 256 * part + 128 * a
                                tiles[ch, part, first(i) + j - i] = found[
                                    top : top + 128, 128 * b : 128 * b + 128
                                ]
            for copy in leaving(ch, pair):
                copy.start()

    def step(ch, _):
        arriving(ch).wait()
        prepare(ch)
        for copy in arriving_old(ch):
            copy.wait()
        multiply(ch)
        return 0

    lax.fori_loop(0, DEVICE_CHANNELS, step, 0)
    for ch in range(DEVICE_CHANNELS):
        for pair in range(ANTENNA_BLOCKS // 2):
            for copy in leaving(ch, pair):
                copy.wait()


def correlate(received, y, left):
    out = jax.ShapeDtypeStruct((DEVICE_CHANNELS, PAIRS, 128, 128), jnp.float32)
    anywhere = pl.BlockSpec(memory_space=pl.ANY)
    right_shape = pltpu.VMEM((DEVICE_CHANNELS, 2 * DEPTH, ANTENNA_COUNT), jnp.bfloat16)
    left_shape = pltpu.VMEM((DEVICE_CHANNELS, 2, ANTENNA_COUNT, 2 * DEPTH), jnp.bfloat16)
    return pl.pallas_call(
        correlate_kernel,
        out_shape=(out, out),
        in_specs=[anywhere] * 3,
        out_specs=(anywhere, anywhere),
        scratch_shapes=[
            pltpu.VMEM(received.shape, jnp.bfloat16),
            right_shape,
            left_shape,
            right_shape,
            left_shape,
            pltpu.VMEM((DEVICE_CHANNELS, 2, PAIRS, 128, 128), jnp.float32),
            pltpu.SemaphoreType.DMA((DEVICE_CHANNELS,)),
            pltpu.SemaphoreType.DMA((DEVICE_CHANNELS, 2)),
            pltpu.SemaphoreType.DMA((DEVICE_CHANNELS, ANTENNA_BLOCKS // 2, 2)),
        ],
        compiler_params=pltpu.CompilerParams(vmem_limit_bytes=60 * 2**20),
        cost_estimate=pl.CostEstimate(flops=5 * 10**9, bytes_accessed=12 * 2**20, transcendentals=0),
    )(received, y, left)


def exchange(departing):
    received = lax.all_to_all(departing, AXES, split_axis=0, concat_axis=0, tiled=True)
    return received.reshape(DEVICES // 2, 2, *received.shape[1:])


def on_device(voltages, taps):
    frames = voltages.reshape(TILE_ANTENNAS, FRAMES, 2, 8, 128).transpose(0, 1, 3, 2, 4)
    frames = frames.reshape(TILE_ANTENNAS, FRAMES, 16, 128)
    high, low = (jnp.asarray(table) for table in transform_tables())
    early = filterbank(frames, taps, high, low, EARLY_UNITS)
    taps, early = lax.optimization_barrier((taps, early))
    late = filterbank(frames, taps, high, low, LATE_UNITS)
    y, left = join(exchange(early))
    return correlate(exchange(late), y, left)


def solution(mesh):
    in_specs = (P(("grp", "tile"), "chan", None, None), P())
    out_specs = (P(AXES, None, None, None), P(AXES, None, None, None))
    return jax.shard_map(
        on_device, mesh=mesh, in_specs=in_specs, out_specs=out_specs, check_vma=False
    )
```

time: 149 us -> 129 us (0.87)
  blocking collectives: 76.1 us -> 0 us
  waiting for transfers between devices: 0 us -> 42 us
  starting transfers between devices: 0 us -> 16.8 us
  Pallas kernels: 70.5 us -> 68.9 us
    all_to_all x1 -> x0, blocking collectives: 76.1 us -> none  [on_device(): lax.all_to_all(departing, AXES, split_axis=0, concat_axis=0, tiled=True)]
    all_to_all x0 -> x2, waiting for transfers between devices: none -> 42 us  [exchange(): lax.all_to_all(departing, AXES, split_axis=0, concat_axis=0, tiled=True)]
    all_to_all x0 -> x2, starting transfers between devices: none -> 16.8 us  [exchange(): lax.all_to_all(departing, AXES, split_axis=0, concat_axis=0, tiled=True)]
    pallas_call x2 -> x4, Pallas kernels: 70.5 us -> 68.9 us  [the longest x2 53.3 us: filterbank(): pl.pallas_call(functools.partial(filterbank_kernel, units, tuple(order)),...]
  transfers between devices with their start and end apart: 0 -> 2, of which waited for: 0 -> 2; matrix products, arithmetic and copies ran while one was open for 0% -> 0% of each run, Pallas kernels for 0% -> 23%
where the time goes in v2:
time: 129 us
  Pallas kernels  68.9 us (53%)
  waiting for transfers between devices  42 us (33%)
  starting transfers between devices  16.8 us (13%)
    pallas_call x2, Pallas kernels, filterbank(): pl.pallas_call(functools.partial(filterbank_kernel, units, tuple(order)),...  53.3 us
    all_to_all x2, waiting for transfers between devices, exchange(): lax.all_to_all(departing, AXES, split_axis=0, concat_axis=0, tiled=True)  42 us
    all_to_all x2, starting transfers between devices, exchange(): lax.all_to_all(departing, AXES, split_axis=0, concat_axis=0, tiled=True)  16.8 us
    pallas_call x1, Pallas kernels, correlate(): pl.pallas_call(correlate_kernel, out_shape=(out, out), in_specs=[anywhere...  10.3 us
    pallas_call x1, Pallas kernels, join(): pl.pallas_call(join_kernel, out_shape=(jax.ShapeDtypeStruct((DEVICE_CHANN...  5.24 us
  transfers between devices with their start and end apart: 2, of which 2 were waited for; matrix products, arithmetic and copies ran while one was open for 0% of the time, Pallas kernels for 23%

profile of v2, /device:TPU:1, one launch (start us, length us, event | category | flops | bytes accessed | tf_op | source)
XLA Modules:
  0.0 128.5 jit_solution(4577248696221459252)
XLA Ops:
  0.6 28.4 %shard_map.59 = bf16[128,2,2,24,128]{4,3,2,1,0:T(8,128)(2,1)} custom-call(bf16[128,32,16,128]{3,2,1,0:T(8,128)(2,1)} %bitcast.8, f32[8,1024]{1,0:T(8,128)} %taps_ref.2, bf16[2,1024,256]{2,1,0:T(8,128)(2,1)} %constant.4.clone.high_hbm, bf16[2,1024,256]{2,1,0:T(8,128)(2,1)} %constant.5.clone.low_hbm), custom_call_target="tpu_custom_call" | custom-call | flops 30000001024 | bytes 20971520 | tf_op jit(solution)/shard_map/pallas_call | solution.py:157
  29.1 11.5 %all-to-all-start.1 = ((bf16[128,2,2,24,128]{4,3,2,1,0:T(8,128)(2,1)}), bf16[128,2,2,24,128]{4,3,2,1,0:T(8,128)(2,1)S(1)}, u32[]{:S(2)}, u32[]{:S(2)}) async-start(bf16[128,2,2,24,128]{4,3,2,1,0:T(8,128)(2,1)} %shard_map.59), calls=%async_computation.1 | async-start | bytes 6291456 | tf_op jit(solution)/shard_map/all_to_all | solution.py:321
  40.6 24.9 %shard_map.60 = bf16[128,2,2,16,128]{4,3,2,1,0:T(8,128)(2,1)} custom-call(bf16[128,32,16,128]{3,2,1,0:T(8,128)(2,1)} %bitcast.9, f32[8,1024]{1,0:T(8,128)} %taps_ref.2, bf16[2,1024,256]{2,1,0:T(8,128)(2,1)} %constant.4.clone.high_hbm, bf16[2,1024,256]{2,1,0:T(8,128)(2,1)} %constant.5.clone.low_hbm), custom_call_target="tpu_custom_call" | custom-call | flops 30000001024 | bytes 20971520 | tf_op jit(solution)/shard_map/pallas_call | solution.py:157
  65.5 16.8 %all-to-all-done.1 = bf16[128,2,2,24,128]{4,3,2,1,0:T(8,128)(2,1)S(1)} async-done(((bf16[128,2,2,24,128]{4,3,2,1,0:T(8,128)(2,1)}), bf16[128,2,2,24,128]{4,3,2,1,0:T(8,128)(2,1)S(1)}, u32[]{:S(2)}, u32[]{:S(2)}) %all-to-all-start.1) | async-done | bytes 3145760 | tf_op jit(solution)/shard_map/all_to_all | solution.py:321
  82.3 0.0 copy-start
  82.3 5.3 %all-to-all-start = ((bf16[128,2,2,16,128]{4,3,2,1,0:T(8,128)(2,1)}), bf16[128,2,2,16,128]{4,3,2,1,0:T(8,128)(2,1)}, u32[]{:S(2)}, u32[]{:S(2)}) async-start(bf16[128,2,2,16,128]{4,3,2,1,0:T(8,128)(2,1)} %shard_map.60), calls=%async_computation | async-start | bytes 4194304 | tf_op jit(solution)/shard_map/all_to_all | solution.py:321
  87.6 0.0 copy-done
  87.6 5.2 %shard_map.61 = (bf16[2,512,1024]{2,1,0:T(8,128)(2,1)}, bf16[2,2,1024,512]{3,2,1,0:T(8,128)(2,1)}) custom-call(bf16[64,2,2,2,24,128]{5,4,3,2,1,0:T(8,128)(2,1)} %bitcast.7), custom_call_target="tpu_custom_call" | custom-call | flops 5000000000 | bytes 12582912 | tf_op jit(solution)/shard_map/pallas_call | solution.py:210
  92.8 25.2 %all-to-all-done = bf16[128,2,2,16,128]{4,3,2,1,0:T(8,128)(2,1)} async-done(((bf16[128,2,2,16,128]{4,3,2,1,0:T(8,128)(2,1)}), bf16[128,2,2,16,128]{4,3,2,1,0:T(8,128)(2,1)}, u32[]{:S(2)}, u32[]{:S(2)}) %all-to-all-start) | async-done | bytes 2097184 | tf_op jit(solution)/shard_map/all_to_all | solution.py:321
  118.0 10.3 %shard_map.62 = (f32[2,36,128,128]{3,2,1,0:T(8,128)}, f32[2,36,128,128]{3,2,1,0:T(8,128)}) custom-call(bf16[64,2,2,2,16,128]{5,4,3,2,1,0:T(8,128)(2,1)} %bitcast.5.in_hbm, bf16[2,512,1024]{2,1,0:T(8,128)(2,1)} %get-tuple-element.8.y_hbm, bf16[2,2,1024,512]{3,2,1,0:T(8,128)(2,1)} %get-tuple-element.9.left_hbm), custom_call_target="tpu_custom_call" | custom-call | flops 5000000000 | bytes 12582912 | tf_op jit(solution)/shard_map/pallas_call | solution.py:299
Async XLA Ops:
  29.1 53.2 %all-to-all-start.1 = ((bf16[128,2,2,24,128]{4,3,2,1,0:T(8,128)(2,1)}), bf16[128,2,2,24,128]{4,3,2,1,0:T(8,128)(2,1)S(1)}, u32[]{:S(2)}, u32[]{:S(2)}) async-start(bf16[128,2,2,24,128]{4,3,2,1,0:T(8,128)(2,1)} %shard_map.59), calls=%async_computation.1 | async-start | bytes 6291456 | tf_op jit(solution)/shard_map/all_to_all | solution.py:321
  82.3 5.3 %copy-start = (bf16[128,2,2,24,128]{4,3,2,1,0:T(8,128)(2,1)}, bf16[128,2,2,24,128]{4,3,2,1,0:T(8,128)(2,1)S(1)}, u32[]{:S(2)}) copy-start(bf16[128,2,2,24,128]{4,3,2,1,0:T(8,128)(2,1)S(1)} %all-to-all-done.1) | copy-start | bytes 9437188
  82.3 35.8 %all-to-all-start = ((bf16[128,2,2,16,128]{4,3,2,1,0:T(8,128)(2,1)}), bf16[128,2,2,16,128]{4,3,2,1,0:T(8,128)(2,1)}, u32[]{:S(2)}, u32[]{:S(2)}) async-start(bf16[128,2,2,16,128]{4,3,2,1,0:T(8,128)(2,1)} %shard_map.60), calls=%async_computation | async-start | bytes 4194304 | tf_op jit(solution)/shard_map/all_to_all | solution.py:321

commit v3 on v2

v3 whole, which is shorter than its diff:
```python
import functools

import jax
import jax.numpy as jnp
import ml_dtypes
import numpy as np
from jax import lax
from jax.experimental import pallas as pl
from jax.experimental.pallas import tpu as pltpu
from jax.sharding import PartitionSpec as P

ANTENNA_COUNT = 1024
FRAME_SAMPLES = 1024
FILTER_TAPS = 8
ANTENNA_BLOCKS = 8
SPECTRA_COUNT = 512
DEVICE_CHANNELS = 2
TILE_ANTENNAS = 128
DEVICES = 128
FRAMES = 32
PIECE = 4
TIME_BLOCKS = 16
PAIRS = ANTENNA_BLOCKS * (ANTENNA_BLOCKS + 1) // 2
HALF = FRAME_SAMPLES // 2
AXES = ("grp", "chan", "tile")

EARLY_UNITS = ((0, 8), (32, 8), (8, 4))
LATE_UNITS = ((16, 8), (24, 8), (12, 4))
OLD_DEPTH = 2 * (8 + 4) * TIME_BLOCKS
DEPTH = 2 * FRAMES * TIME_BLOCKS


def transform_tables():
    sample = np.arange(HALF)
    parts = []
    for odd in range(2):
        channel = 2 * np.arange(DEVICES) + odd
        angle = 2.0 * np.pi * ((sample[:, None] * channel[None, :]) % FRAME_SAMPLES) / FRAME_SAMPLES
        cosine, sine = np.cos(angle), np.sin(angle)
        from_real = np.concatenate([cosine, -sine], axis=1)
        from_imag = np.concatenate([sine, cosine], axis=1)
        both = np.stack([from_real.reshape(4, 128, 256), from_imag.reshape(4, 128, 256)], axis=1)
        parts.append(both.reshape(FRAME_SAMPLES, 256))
    table = np.stack(parts).astype(np.float32)
    high = table.astype(ml_dtypes.bfloat16)
    low = (table - high.astype(np.float32)).astype(ml_dtypes.bfloat16)
    return high, low


def filterbank_kernel(units, order, x_hbm, taps_ref, high_hbm, low_hbm, out_hbm, *scratch):
    x_v, taps_rows, high_ref, low_ref, z, spectra, out_v, x_sems, table_sems, out_sems = scratch
    slot = {piece: i for i, piece in enumerate(order)}
    copies = [
        pltpu.make_async_copy(
            x_hbm.at[:, pl.ds(PIECE * piece, PIECE)], x_v.at[:, pl.ds(PIECE * i, PIECE)], x_sems.at[i]
        )
        for i, piece in enumerate(order)
    ]
    tables = [
        pltpu.make_async_copy(high_hbm, high_ref, table_sems.at[0]),
        pltpu.make_async_copy(low_hbm, low_ref, table_sems.at[1]),
    ]
    for copy in copies[:2] + tables + copies[2:]:
        copy.start()
    for k in range(FILTER_TAPS):
        for j in range(8):
            row = taps_ref[k : k + 1, 128 * j : 128 * j + 128]
            taps_rows[k, 2 * j : 2 * j + 2, :] = jnp.broadcast_to(row, (2, 128))

    def inputs(start, count):
        return [s for s in range(start - FILTER_TAPS + 1, start + count) if 0 <= s < FRAMES]

    def filter_antenna(start, count, a):
        frames = {
            s: x_v[a, slot[s // PIECE] * PIECE + s % PIECE].astype(jnp.float32)
            for s in inputs(start, count)
        }
        rows = pl.ds(pl.multiple_of(a * 8, 8), 8)
        for q in range(count):
            total = None
            for k in range(FILTER_TAPS):
                s = start + q - k
                if s in frames:
                    term = taps_rows[k] * frames[s]
                    total = term if total is None else total + term
            if total is None:
                total = jnp.zeros((16, 128), jnp.float32)
            z[0, q, rows, :] = total[:8] + total[8:]
            z[1, q, rows, :] = total[:8] - total[8:]

    def transform(count, top, odd):
        highs, lows = [], []
        for row in range(8):
            piece = jnp.concatenate(
                [z[odd, e, pl.ds(row, TILE_ANTENNAS, stride=8), :] for e in range(count)], axis=0
            )
            high = piece.astype(jnp.bfloat16)
            highs.append(high)
            lows.append((piece - high.astype(jnp.float32)).astype(jnp.bfloat16))
        high = jnp.concatenate(highs, axis=1)
        low = jnp.concatenate(lows, axis=1)
        size = count * TILE_ANTENNAS
        dot = functools.partial(jnp.dot, preferred_element_type=jnp.float32)
        both = dot(jnp.concatenate([high, low], axis=0), high_ref[odd])
        found = (both[:size] + both[size:] + dot(high, low_ref[odd])).T
        step = 1024 if count == 8 else 4
        for part in range(2):
            for e in range(count):
                spectra[pl.ds(step * part + e, DEVICES, stride=8), :] = found[
                    128 * part : 128 * part + 128, 128 * e : 128 * e + 128
                ]
        for n in range(count // 4):
            rows = spectra[1024 * n : 1024 * (n + 1), :].reshape(DEVICES, 8, 128)
            place = top + 2 * count * odd + 8 * n
            out_v[:, place : place + 8, :] = rows.astype(jnp.bfloat16)

    waited = 0
    top = 0
    leaving = []
    for u, (start, count) in enumerate(units):
        last = max(slot[s // PIECE] for s in inputs(start, count))
        while waited <= last:
            copies[waited].wait()
            waited += 1

        def filter_step(a, _, start=start, count=count):
            filter_antenna(start, count, a)
            return 0

        lax.fori_loop(0, TILE_ANTENNAS, filter_step, 0, unroll=2)
        if u == 0:
            for copy in tables:
                copy.wait()
        for odd in range(2):
            transform(count, top, odd)
        rows = pl.ds(top, 4 * count)
        copy = pltpu.make_async_copy(out_v.at[:, rows], out_hbm.at[:, rows], out_sems.at[u])
        copy.start()
        leaving.append(copy)
        top += 4 * count
    for copy in leaving:
        copy.wait()


def filterbank(frames, taps, high, low, units):
    order = []
    for start, count in units:
        for s in range(start - FILTER_TAPS + 1, start + count):
            if 0 <= s < FRAMES and s // PIECE not in order:
                order.append(s // PIECE)
    anywhere = pl.BlockSpec(memory_space=pl.ANY)
    shape = (DEVICES, 4 * sum(count for _, count in units), 128)
    table = pltpu.VMEM((2, FRAME_SAMPLES, 256), jnp.bfloat16)
    return pl.pallas_call(
        functools.partial(filterbank_kernel, units, tuple(order)),
        out_shape=jax.ShapeDtypeStruct(shape, jnp.bfloat16),
        in_specs=[anywhere, pl.BlockSpec(memory_space=pltpu.VMEM), anywhere, anywhere],
        out_specs=anywhere,
        scratch_shapes=[
            pltpu.VMEM((TILE_ANTENNAS, PIECE * len(order), 16, 128), jnp.bfloat16),
            pltpu.VMEM((FILTER_TAPS, 16, 128), jnp.float32),
            table,
            table,
            pltpu.VMEM((2, 8, 1024, 128), jnp.float32),
            pltpu.VMEM((2048, 128), jnp.float32),
            pltpu.VMEM(shape, jnp.bfloat16),
            pltpu.SemaphoreType.DMA((len(order),)),
            pltpu.SemaphoreType.DMA((2,)),
            pltpu.SemaphoreType.DMA((len(units),)),
        ],
        compiler_params=pltpu.CompilerParams(vmem_limit_bytes=60 * 2**20),
        cost_estimate=pl.CostEstimate(flops=30 * 10**9, bytes_accessed=20 * 2**20, transcendentals=0),
    )(frames, taps, high, low)


def store_eight(y, left, b, depth, real, imag):
    rows, half, end = slice(128 * b, 128 * b + 128), depth + 128, depth + 256
    parts = [part.reshape(8 * TIME_BLOCKS, 128).astype(jnp.bfloat16) for part in (real, imag)]
    block = jnp.concatenate(parts, axis=0)
    turned = block.T
    y[depth:end, rows] = block
    left[0, rows, depth:end] = turned
    left[1, rows, depth:half] = turned[:, 128:]
    left[1, rows, half:end] = -turned[:, :128]


def store_four(y, left, b, depth, both):
    rows, end = slice(128 * b, 128 * b + 128), depth + 128
    swapped = jnp.concatenate([both[:, 4:], -both[:, :4]], axis=1)
    block, swapped = (
        part.reshape(8 * TIME_BLOCKS, 128).astype(jnp.bfloat16) for part in (both, swapped)
    )
    y[depth:end, rows] = block
    left[0, rows, depth:end] = block.T
    left[1, rows, depth:end] = swapped.T


def join_kernel(in_ref, y, left):
    for ch in range(DEVICE_CHANNELS):
        for b in range(ANTENNA_BLOCKS):
            sources, tile = pl.ds((b // 2) * TIME_BLOCKS, TIME_BLOCKS), b % 2

            def eight(row):
                return in_ref[sources, tile, row : row + 8, :].astype(jnp.float32)

            parts = []
            for part in range(2):
                tail = eight(32 + 16 * ch + 8 * part)
                none = jnp.zeros((1, 8, 128), jnp.float32)
                parts.append(eight(16 * ch + 8 * part) + jnp.concatenate([none, tail[:-1]], axis=0))
            store_eight(y.at[ch], left.at[ch], b, 0, *parts)
            store_four(y.at[ch], left.at[ch], b, 256, eight(64 + 8 * ch))


def join(received):
    vmem = pl.BlockSpec(memory_space=pltpu.VMEM)
    return pl.pallas_call(
        join_kernel,
        out_shape=(
            jax.ShapeDtypeStruct((DEVICE_CHANNELS, OLD_DEPTH, ANTENNA_COUNT), jnp.bfloat16),
            jax.ShapeDtypeStruct((DEVICE_CHANNELS, 2, ANTENNA_COUNT, OLD_DEPTH), jnp.bfloat16),
        ),
        in_specs=[vmem],
        out_specs=(vmem, vmem),
        compiler_params=pltpu.CompilerParams(vmem_limit_bytes=24 * 2**20),
        cost_estimate=pl.CostEstimate(flops=5 * 10**9, bytes_accessed=12 * 2**20, transcendentals=0),
    )(received)


def correlate_kernel(in_hbm, y_hbm, left_hbm, real_hbm, imag_hbm, *scratch):
    in_ref, y, left, tiles, in_sem, old_sems, out_sems = scratch
    arriving = pltpu.make_async_copy(in_hbm, in_ref, in_sem)

    def arriving_old(ch):
        old = pl.ds(0, OLD_DEPTH)
        return (
            pltpu.make_async_copy(y_hbm.at[ch], y.at[ch, old], old_sems.at[ch, 0]),
            pltpu.make_async_copy(left_hbm.at[ch], left.at[ch, :, :, old], old_sems.at[ch, 1]),
        )

    arriving.start()
    for ch in range(DEVICE_CHANNELS):
        for copy in arriving_old(ch):
            copy.start()
    dot = functools.partial(jnp.dot, preferred_element_type=jnp.float32)

    def first(i):
        return ANTENNA_BLOCKS * i - i * (i - 1) // 2

    def prepare(ch):
        for b in range(ANTENNA_BLOCKS):
            sources, tile = pl.ds((b // 2) * TIME_BLOCKS, TIME_BLOCKS), b % 2

            def eight(row):
                return in_ref[sources, tile, row : row + 8, :].astype(jnp.float32)

            for unit in range(2):
                row = 32 * unit + 16 * ch
                store_eight(y.at[ch], left.at[ch], b, OLD_DEPTH + 256 * unit, eight(row), eight(row + 8))
            store_four(y.at[ch], left.at[ch], b, OLD_DEPTH + 512, eight(64 + 8 * ch))

    def leaving(ch, pair):
        some = pl.ds(first(2 * pair), first(2 * pair + 2) - first(2 * pair))
        return [
            pltpu.make_async_copy(tiles.at[ch, part, some], ref.at[ch, some], out_sems.at[ch, pair, part])
            for part, ref in enumerate((real_hbm, imag_hbm))
        ]

    def multiply(ch):
        for pair in range(ANTENNA_BLOCKS // 2):
            rows = pl.ds(256 * pair, 256)
            lhs = left[ch, :, rows, :].reshape(512, DEPTH)
            for other in range(pair, ANTENNA_BLOCKS // 2):
                columns = pl.ds(256 * other, 256)
                found = dot(lhs, y[ch, :, columns]) * (1.0 / SPECTRA_COUNT)
                for a in range(2):
                    for b in range(2):
                        i, j = 2 * pair + a, 2 * other + b
                        if i <= j:
                            for part in range(2):
                                top = 256 * part + 128 * a
                                tiles[ch, part, first(i) + j - i] = found[
                                    top : top + 128, 128 * b : 128 * b + 128
                                ]
            for copy in leaving(ch, pair):
                copy.start()

    def step(ch, _):
        for copy in arriving_old(ch):
            copy.wait()
        multiply(ch)
        return 0

    arriving.wait()
    for ch in range(DEVICE_CHANNELS):
        prepare(ch)
    lax.fori_loop(0, DEVICE_CHANNELS, step, 0)
    for ch in range(DEVICE_CHANNELS):
        for pair in range(ANTENNA_BLOCKS // 2):
            for copy in leaving(ch, pair):
                copy.wait()


def correlate(received, y, left):
    out = jax.ShapeDtypeStruct((DEVICE_CHANNELS, PAIRS, 128, 128), jnp.float32)
    anywhere = pl.BlockSpec(memory_space=pl.ANY)
    return pl.pallas_call(
        correlate_kernel,
        out_shape=(out, out),
        in_specs=[anywhere] * 3,
        out_specs=(anywhere, anywhere),
        scratch_shapes=[
            pltpu.VMEM(received.shape, jnp.bfloat16),
            pltpu.VMEM((DEVICE_CHANNELS, DEPTH, ANTENNA_COUNT), jnp.bfloat16),
            pltpu.VMEM((DEVICE_CHANNELS, 2, ANTENNA_COUNT, DEPTH), jnp.bfloat16),
            pltpu.VMEM((DEVICE_CHANNELS, 2, PAIRS, 128, 128), jnp.float32),
            pltpu.SemaphoreType.DMA,
            pltpu.SemaphoreType.DMA((DEVICE_CHANNELS, 2)),
            pltpu.SemaphoreType.DMA((DEVICE_CHANNELS, ANTENNA_BLOCKS // 2, 2)),
        ],
        compiler_params=pltpu.CompilerParams(vmem_limit_bytes=60 * 2**20),
        cost_estimate=pl.CostEstimate(flops=5 * 10**9, bytes_accessed=12 * 2**20, transcendentals=0),
    )(received, y, left)


def exchange(departing):
    received = lax.all_to_all(departing, AXES, split_axis=0, concat_axis=0, tiled=True)
    return received.reshape(DEVICES // 2, 2, *received.shape[1:])


def on_device(voltages, taps):
    frames = voltages.reshape(TILE_ANTENNAS, FRAMES, 2, 8, 128).transpose(0, 1, 3, 2, 4)
    frames = frames.reshape(TILE_ANTENNAS, FRAMES, 16, 128)
    high, low = (jnp.asarray(table) for table in transform_tables())
    early = filterbank(frames, taps, high, low, EARLY_UNITS)
    taps, early = lax.optimization_barrier((taps, early))
    late = filterbank(frames, taps, high, low, LATE_UNITS)
    y, left = join(exchange(early))
    return correlate(exchange(late), y, left)


def solution(mesh):
    in_specs = (P(("grp", "tile"), "chan", None, None), P())
    out_specs = (P(AXES, None, None, None), P(AXES, None, None, None))
    return jax.shard_map(
        on_device, mesh=mesh, in_specs=in_specs, out_specs=out_specs, check_vma=False
    )
```

time: 129 us -> 125 us (0.969)
  Pallas kernels: 68.9 us -> 65.6 us
  waiting for transfers between devices: 42 us -> 38.7 us
  local copies, waits for them, and re-layouts: 0.01 us -> 2.82 us
    pallas_call x1, Pallas kernels: 5.24 us -> 0.79 us  [join(): pl.pallas_call(join_kernel, out_shape=(jax.ShapeDtypeStruct((DEVICE_CHANN...]
    all_to_all x2, waiting for transfers between devices: 42 us -> 38.7 us  [exchange(): lax.all_to_all(departing, AXES, split_axis=0, concat_axis=0, tiled=True)]
    unnamed x2 -> x4, local copies, waits for them, and re-layouts: 0.01 us -> 2.82 us
  transfers between devices with their start and end apart: 2 -> 2, of which waited for: 2 -> 2; matrix products, arithmetic and copies ran while one was open for 0% -> 0% of each run, Pallas kernels for 23% -> 25%
where the time goes in v3:
time: 125 us; the launch traced here: 124 us
  Pallas kernels  65.6 us (52%)
  waiting for transfers between devices  38.7 us (31%)
  starting transfers between devices  16.6 us (13%)
  local copies, waits for them, and re-layouts  2.82 us (2%)
    pallas_call x2, Pallas kernels, filterbank(): pl.pallas_call(functools.partial(filterbank_kernel, units, tuple(order)),...  53.6 us
    all_to_all x2, waiting for transfers between devices, exchange(): lax.all_to_all(departing, AXES, split_axis=0, concat_axis=0, tiled=True)  38.7 us
    all_to_all x2, starting transfers between devices, exchange(): lax.all_to_all(departing, AXES, split_axis=0, concat_axis=0, tiled=True)  16.6 us
    pallas_call x1, Pallas kernels, correlate(): pl.pallas_call(correlate_kernel, out_shape=(out, out), in_specs=[anywhere...  11.2 us
    unnamed x4, local copies, waits for them, and re-layouts  2.82 us
  transfers between devices with their start and end apart: 2, of which 2 were waited for; matrix products, arithmetic and copies ran while one was open for 0% of the time, Pallas kernels for 25%

profile of v3, /device:TPU:1, one launch (start us, length us, event | category | flops | bytes accessed | tf_op | source)
XLA Modules:
  0.0 124.5 jit_solution(12962124676369425484)
XLA Ops:
  0.6 23.6 %shard_map.59 = bf16[128,80,128]{2,1,0:T(8,128)(2,1)} custom-call(bf16[128,32,16,128]{3,2,1,0:T(8,128)(2,1)} %bitcast.8, f32[8,1024]{1,0:T(8,128)} %taps_ref.2, bf16[2,1024,256]{2,1,0:T(8,128)(2,1)} %constant.4.clone.high_hbm, bf16[2,1024,256]{2,1,0:T(8,128)(2,1)} %constant.5.clone.low_hbm), custom_call_target="tpu_custom_call" | custom-call | flops 30000001024 | bytes 20971520 | tf_op jit(solution)/shard_map/pallas_call | solution.py:154
  24.2 11.5 %all-to-all-start.1 = ((bf16[128,80,128]{2,1,0:T(8,128)(2,1)}), bf16[128,80,128]{2,1,0:T(8,128)(2,1)S(1)}, u32[]{:S(2)}, u32[]{:S(2)}) async-start(bf16[128,80,128]{2,1,0:T(8,128)(2,1)} %shard_map.59), calls=%async_computation.1 | async-start | bytes 5242880 | tf_op jit(solution)/shard_map/all_to_all | solution.py:327
  35.7 30.0 %shard_map.60 = bf16[128,80,128]{2,1,0:T(8,128)(2,1)} custom-call(bf16[128,32,16,128]{3,2,1,0:T(8,128)(2,1)} %bitcast.9, f32[8,1024]{1,0:T(8,128)} %taps_ref.2, bf16[2,1024,256]{2,1,0:T(8,128)(2,1)} %constant.4.clone.high_hbm, bf16[2,1024,256]{2,1,0:T(8,128)(2,1)} %constant.5.clone.low_hbm), custom_call_target="tpu_custom_call" | custom-call | flops 30000001024 | bytes 20971520 | tf_op jit(solution)/shard_map/pallas_call | solution.py:154
  65.7 6.2 %all-to-all-done.1 = bf16[128,80,128]{2,1,0:T(8,128)(2,1)S(1)} async-done(((bf16[128,80,128]{2,1,0:T(8,128)(2,1)}), bf16[128,80,128]{2,1,0:T(8,128)(2,1)S(1)}, u32[]{:S(2)}, u32[]{:S(2)}) %all-to-all-start.1) | async-done | bytes 2621472 | tf_op jit(solution)/shard_map/all_to_all | solution.py:327
  72.0 5.1 %all-to-all-start = ((bf16[128,80,128]{2,1,0:T(8,128)(2,1)}), bf16[128,80,128]{2,1,0:T(8,128)(2,1)}, u32[]{:S(2)}, u32[]{:S(2)}) async-start(bf16[128,80,128]{2,1,0:T(8,128)(2,1)} %shard_map.60), calls=%async_computation | async-start | bytes 5242880 | tf_op jit(solution)/shard_map/all_to_all | solution.py:327
  77.0 0.8 shard_map.61
  77.8 0.0 copy-start
  77.8 1.6 %copy-done = bf16[2,2,1024,384]{3,2,1,0:T(8,128)(2,1)} copy-done((bf16[2,2,1024,384]{3,2,1,0:T(8,128)(2,1)}, bf16[2,2,1024,384]{3,2,1,0:T(8,128)(2,1)S(1)}, u32[]{:S(2)}) %copy-start) | copy-done | bytes 3145752
  79.5 0.0 copy-start.1
  79.5 1.2 copy-done.1
  80.7 32.4 %all-to-all-done = bf16[128,80,128]{2,1,0:T(8,128)(2,1)} async-done(((bf16[128,80,128]{2,1,0:T(8,128)(2,1)}), bf16[128,80,128]{2,1,0:T(8,128)(2,1)}, u32[]{:S(2)}, u32[]{:S(2)}) %all-to-all-start) | async-done | bytes 2621472 | tf_op jit(solution)/shard_map/all_to_all | solution.py:327
  113.1 11.2 %shard_map.62 = (f32[2,36,128,128]{3,2,1,0:T(8,128)}, f32[2,36,128,128]{3,2,1,0:T(8,128)}) custom-call(bf16[64,2,80,128]{3,2,1,0:T(8,128)(2,1)} %bitcast.5.in_hbm, bf16[2,384,1024]{2,1,0:T(8,128)(2,1)} %copy-done.1, bf16[2,2,1024,384]{3,2,1,0:T(8,128)(2,1)} %copy-done), custom_call_target="tpu_custom_call" | custom-call | flops 5000000000 | bytes 12582912 | tf_op jit(solution)/shard_map/pallas_call | solution.py:307
Async XLA Ops:
  24.2 47.7 %all-to-all-start.1 = ((bf16[128,80,128]{2,1,0:T(8,128)(2,1)}), bf16[128,80,128]{2,1,0:T(8,128)(2,1)S(1)}, u32[]{:S(2)}, u32[]{:S(2)}) async-start(bf16[128,80,128]{2,1,0:T(8,128)(2,1)} %shard_map.59), calls=%async_computation.1 | async-start | bytes 5242880 | tf_op jit(solution)/shard_map/all_to_all | solution.py:327
  72.0 41.1 %all-to-all-start = ((bf16[128,80,128]{2,1,0:T(8,128)(2,1)}), bf16[128,80,128]{2,1,0:T(8,128)(2,1)}, u32[]{:S(2)}, u32[]{:S(2)}) async-start(bf16[128,80,128]{2,1,0:T(8,128)(2,1)} %shard_map.60), calls=%async_computation | async-start | bytes 5242880 | tf_op jit(solution)/shard_map/all_to_all | solution.py:327
  77.8 1.7 %copy-start = (bf16[2,2,1024,384]{3,2,1,0:T(8,128)(2,1)}, bf16[2,2,1024,384]{3,2,1,0:T(8,128)(2,1)S(1)}, u32[]{:S(2)}) copy-start(bf16[2,2,1024,384]{3,2,1,0:T(8,128)(2,1)S(1)} %get-tuple-element.9.left_hbm) | copy-start | bytes 9437188
  79.5 1.2 copy-start.1

commit v4 on v3

--- a/solution.py
+++ b/solution.py
@@ -23,6 +23,8 @@
 PAIRS = ANTENNA_BLOCKS * (ANTENNA_BLOCKS + 1) // 2
 HALF = FRAME_SAMPLES // 2
 AXES = ("grp", "chan", "tile")
+SHARES = 4
+SHARE = TILE_ANTENNAS // SHARES
 
 EARLY_UNITS = ((0, 8), (32, 8), (8, 4))
 LATE_UNITS = ((16, 8), (24, 8), (12, 4))
@@ -50,18 +52,27 @@
 def filterbank_kernel(units, order, x_hbm, taps_ref, high_hbm, low_hbm, out_hbm, *scratch):
     x_v, taps_rows, high_ref, low_ref, z, spectra, out_v, x_sems, table_sems, out_sems = scratch
     slot = {piece: i for i, piece in enumerate(order)}
-    copies = [
-        pltpu.make_async_copy(
-            x_hbm.at[:, pl.ds(PIECE * piece, PIECE)], x_v.at[:, pl.ds(PIECE * i, PIECE)], x_sems.at[i]
+
+    def arriving(i, share):
+        antennas = pl.ds(SHARE * share, SHARE)
+        return pltpu.make_async_copy(
+            x_hbm.at[antennas, pl.ds(PIECE * order[i], PIECE)],
+            x_v.at[antennas, pl.ds(PIECE * i, PIECE)],
+            x_sems.at[i, share],
         )
-        for i, piece in enumerate(order)
-    ]
+
     tables = [
         pltpu.make_async_copy(high_hbm, high_ref, table_sems.at[0]),
         pltpu.make_async_copy(low_hbm, low_ref, table_sems.at[1]),
     ]
-    for copy in copies[:2] + tables + copies[2:]:
+    for share in range(SHARES):
+        for i in range(2):
+            arriving(i, share).start()
+    for copy in tables:
         copy.start()
+    for i in range(2, len(order)):
+        for share in range(SHARES):
+            arriving(i, share).start()
     for k in range(FILTER_TAPS):
         for j in range(8):
             row = taps_ref[k : k + 1, 128 * j : 128 * j + 128]
@@ -70,12 +81,13 @@
     def inputs(start, count):
         return [s for s in range(start - FILTER_TAPS + 1, start + count) if 0 <= s < FRAMES]
 
-    def filter_antenna(start, count, a):
+    def filter_antenna(start, count, group, k8):
+        a = group * 8 + k8
         frames = {
             s: x_v[a, slot[s // PIECE] * PIECE + s % PIECE].astype(jnp.float32)
             for s in inputs(start, count)
         }
-        rows = pl.ds(pl.multiple_of(a * 8, 8), 8)
+        rows = pl.ds(pl.multiple_of(group * 64, 64) + k8, 8, stride=8)
         for q in range(count):
             total = None
             for k in range(FILTER_TAPS):
@@ -92,7 +104,11 @@
         highs, lows = [], []
         for row in range(8):
             piece = jnp.concatenate(
-                [z[odd, e, pl.ds(row, TILE_ANTENNAS, stride=8), :] for e in range(count)], axis=0
+                [
+                    z[odd, e].reshape(TILE_ANTENNAS // 8, 8, 8, 128)[:, row].reshape(TILE_ANTENNAS, 128)
+                    for e in range(count)
+                ],
+                axis=0,
             )
             high = piece.astype(jnp.bfloat16)
             highs.append(high)
@@ -119,15 +135,23 @@
     leaving = []
     for u, (start, count) in enumerate(units):
         last = max(slot[s // PIECE] for s in inputs(start, count))
-        while waited <= last:
-            copies[waited].wait()
-            waited += 1
-
-        def filter_step(a, _, start=start, count=count):
-            filter_antenna(start, count, a)
+
+        def filter_step(group, _, start=start, count=count):
+            for k8 in range(8):
+                filter_antenna(start, count, group, k8)
             return 0
 
-        lax.fori_loop(0, TILE_ANTENNAS, filter_step, 0, unroll=2)
+        def filter_share(share, _, last=last, waited=waited, filter_step=filter_step):
+            for i in range(waited, last + 1):
+                arriving(i, share).wait()
+            lax.fori_loop(0, SHARE // 8, lambda n, c: filter_step(SHARE // 8 * share + n, c), 0)
+            return 0
+
+        if waited <= last:
+            lax.fori_loop(0, SHARES, filter_share, 0)
+            waited = last + 1
+        else:
+            lax.fori_loop(0, TILE_ANTENNAS // 8, filter_step, 0)
         if u == 0:
             for copy in tables:
                 copy.wait()
@@ -164,7 +188,7 @@
             pltpu.VMEM((2, 8, 1024, 128), jnp.float32),
             pltpu.VMEM((2048, 128), jnp.float32),
             pltpu.VMEM(shape, jnp.bfloat16),
-            pltpu.SemaphoreType.DMA((len(order),)),
+            pltpu.SemaphoreType.DMA((len(order), SHARES)),
             pltpu.SemaphoreType.DMA((2,)),
             pltpu.SemaphoreType.DMA((len(units),)),
         ],
@@ -228,8 +252,16 @@
 
 
 def correlate_kernel(in_hbm, y_hbm, left_hbm, real_hbm, imag_hbm, *scratch):
-    in_ref, y, left, tiles, in_sem, old_sems, out_sems = scratch
-    arriving = pltpu.make_async_copy(in_hbm, in_ref, in_sem)
+    in_ref, y, left, tiles, in_sems, old_sems, out_sems = scratch
+
+    def arriving(ch):
+        tops = (0, 32, 64) if ch == 0 else (16, 48)
+        return [
+            pltpu.make_async_copy(
+                in_hbm.at[:, :, pl.ds(top, 16)], in_ref.at[:, :, pl.ds(top, 16)], in_sems.at[top // 16]
+            )
+            for top in tops
+        ]
 
     def arriving_old(ch):
         old = pl.ds(0, OLD_DEPTH)
@@ -238,9 +270,8 @@
             pltpu.make_async_copy(left_hbm.at[ch], left.at[ch, :, :, old], old_sems.at[ch, 1]),
         )
 
-    arriving.start()
     for ch in range(DEVICE_CHANNELS):
-        for copy in arriving_old(ch):
+        for copy in (*arriving(ch), *arriving_old(ch)):
             copy.start()
     dot = functools.partial(jnp.dot, preferred_element_type=jnp.float32)
 
@@ -285,16 +316,13 @@
             for copy in leaving(ch, pair):
                 copy.start()
 
-    def step(ch, _):
+    for ch in range(DEVICE_CHANNELS):
+        for copy in arriving(ch):
+            copy.wait()
+        prepare(ch)
         for copy in arriving_old(ch):
             copy.wait()
         multiply(ch)
-        return 0
-
-    arriving.wait()
-    for ch in range(DEVICE_CHANNELS):
-        prepare(ch)
-    lax.fori_loop(0, DEVICE_CHANNELS, step, 0)
     for ch in range(DEVICE_CHANNELS):
         for pair in range(ANTENNA_BLOCKS // 2):
             for copy in leaving(ch, pair):
@@ -314,7 +342,7 @@
             pltpu.VMEM((DEVICE_CHANNELS, DEPTH, ANTENNA_COUNT), jnp.bfloat16),
             pltpu.VMEM((DEVICE_CHANNELS, 2, ANTENNA_COUNT, DEPTH), jnp.bfloat16),
             pltpu.VMEM((DEVICE_CHANNELS, 2, PAIRS, 128, 128), jnp.float32),
-            pltpu.SemaphoreType.DMA,
+            pltpu.SemaphoreType.DMA((5,)),
             pltpu.SemaphoreType.DMA((DEVICE_CHANNELS, 2)),
             pltpu.SemaphoreType.DMA((DEVICE_CHANNELS, ANTENNA_BLOCKS // 2, 2)),
         ],

time: 125 us -> 122 us (0.976)
  Pallas kernels: 65.6 us -> 61.1 us
  waiting for transfers between devices: 38.7 us -> 40.8 us
    pallas_call x2, Pallas kernels: 53.6 us -> 50.1 us  [filterbank(): pl.pallas_call(functools.partial(filterbank_kernel, units, tuple(order)),...]
    all_to_all x2, waiting for transfers between devices: 38.7 us -> 40.8 us  [exchange(): lax.all_to_all(departing, AXES, split_axis=0, concat_axis=0, tiled=True)]
  transfers between devices with their start and end apart: 2 -> 2, of which waited for: 2 -> 2; matrix products, arithmetic and copies ran while one was open for 0% -> 0% of each run, Pallas kernels for 25% -> 24%
where the time goes in v4:
time: 122 us
  Pallas kernels  61.1 us (50%)
  waiting for transfers between devices  40.8 us (33%)
  starting transfers between devices  16.6 us (14%)
  local copies, waits for them, and re-layouts  2.82 us (2%)
    pallas_call x2, Pallas kernels, filterbank(): pl.pallas_call(functools.partial(filterbank_kernel, units, tuple(order)),...  50.1 us
    all_to_all x2, waiting for transfers between devices, exchange(): lax.all_to_all(departing, AXES, split_axis=0, concat_axis=0, tiled=True)  40.8 us
    all_to_all x2, starting transfers between devices, exchange(): lax.all_to_all(departing, AXES, split_axis=0, concat_axis=0, tiled=True)  16.6 us
    pallas_call x1, Pallas kernels, correlate(): pl.pallas_call(correlate_kernel, out_shape=(out, out), in_specs=[anywhere...  10.2 us
    unnamed x4, local copies, waits for them, and re-layouts  2.82 us
  transfers between devices with their start and end apart: 2, of which 2 were waited for; matrix products, arithmetic and copies ran while one was open for 0% of the time, Pallas kernels for 24%

profile of v4, /device:TPU:1, one launch (start us, length us, event | category | flops | bytes accessed | tf_op | source)
XLA Modules:
  0.0 122.1 jit_solution(14694379898558994245)
XLA Ops:
  0.6 22.2 %shard_map.59 = bf16[128,80,128]{2,1,0:T(8,128)(2,1)} custom-call(bf16[128,32,16,128]{3,2,1,0:T(8,128)(2,1)} %bitcast.8, f32[8,1024]{1,0:T(8,128)} %taps_ref.2, bf16[2,1024,256]{2,1,0:T(8,128)(2,1)} %constant.4.clone.high_hbm, bf16[2,1024,256]{2,1,0:T(8,128)(2,1)} %constant.5.clone.low_hbm), custom_call_target="tpu_custom_call" | custom-call | flops 30000001024 | bytes 20971520 | tf_op jit(solution)/shard_map/pallas_call | solution.py:178
  22.8 11.5 %all-to-all-start.1 = ((bf16[128,80,128]{2,1,0:T(8,128)(2,1)}), bf16[128,80,128]{2,1,0:T(8,128)(2,1)S(1)}, u32[]{:S(2)}, u32[]{:S(2)}) async-start(bf16[128,80,128]{2,1,0:T(8,128)(2,1)} %shard_map.59), calls=%async_computation.1 | async-start | bytes 5242880 | tf_op jit(solution)/shard_map/all_to_all | solution.py:355
  34.4 27.9 %shard_map.60 = bf16[128,80,128]{2,1,0:T(8,128)(2,1)} custom-call(bf16[128,32,16,128]{3,2,1,0:T(8,128)(2,1)} %bitcast.9, f32[8,1024]{1,0:T(8,128)} %taps_ref.2, bf16[2,1024,256]{2,1,0:T(8,128)(2,1)} %constant.4.clone.high_hbm, bf16[2,1024,256]{2,1,0:T(8,128)(2,1)} %constant.5.clone.low_hbm), custom_call_target="tpu_custom_call" | custom-call | flops 30000001024 | bytes 20971520 | tf_op jit(solution)/shard_map/pallas_call | solution.py:178
  62.3 8.3 %all-to-all-done.1 = bf16[128,80,128]{2,1,0:T(8,128)(2,1)S(1)} async-done(((bf16[128,80,128]{2,1,0:T(8,128)(2,1)}), bf16[128,80,128]{2,1,0:T(8,128)(2,1)S(1)}, u32[]{:S(2)}, u32[]{:S(2)}) %all-to-all-start.1) | async-done | bytes 2621472 | tf_op jit(solution)/shard_map/all_to_all | solution.py:355
  70.6 5.1 %all-to-all-start = ((bf16[128,80,128]{2,1,0:T(8,128)(2,1)}), bf16[128,80,128]{2,1,0:T(8,128)(2,1)}, u32[]{:S(2)}, u32[]{:S(2)}) async-start(bf16[128,80,128]{2,1,0:T(8,128)(2,1)} %shard_map.60), calls=%async_computation | async-start | bytes 5242880 | tf_op jit(solution)/shard_map/all_to_all | solution.py:355
  75.7 0.8 shard_map.61
  76.5 0.0 copy-start
  76.5 1.6 %copy-done = bf16[2,2,1024,384]{3,2,1,0:T(8,128)(2,1)} copy-done((bf16[2,2,1024,384]{3,2,1,0:T(8,128)(2,1)}, bf16[2,2,1024,384]{3,2,1,0:T(8,128)(2,1)S(1)}, u32[]{:S(2)}) %copy-start) | copy-done | bytes 3145752
  78.1 0.0 copy-start.1
  78.1 1.2 copy-done.1
  79.3 32.4 %all-to-all-done = bf16[128,80,128]{2,1,0:T(8,128)(2,1)} async-done(((bf16[128,80,128]{2,1,0:T(8,128)(2,1)}), bf16[128,80,128]{2,1,0:T(8,128)(2,1)}, u32[]{:S(2)}, u32[]{:S(2)}) %all-to-all-start) | async-done | bytes 2621472 | tf_op jit(solution)/shard_map/all_to_all | solution.py:355
  111.7 10.2 %shard_map.62 = (f32[2,36,128,128]{3,2,1,0:T(8,128)}, f32[2,36,128,128]{3,2,1,0:T(8,128)}) custom-call(bf16[64,2,80,128]{3,2,1,0:T(8,128)(2,1)} %bitcast.5.in_hbm, bf16[2,384,1024]{2,1,0:T(8,128)(2,1)} %copy-done.1, bf16[2,2,1024,384]{3,2,1,0:T(8,128)(2,1)} %copy-done), custom_call_target="tpu_custom_call" | custom-call | flops 5000000000 | bytes 12582912 | tf_op jit(solution)/shard_map/pallas_call | solution.py:335
Async XLA Ops:
  22.8 47.7 %all-to-all-start.1 = ((bf16[128,80,128]{2,1,0:T(8,128)(2,1)}), bf16[128,80,128]{2,1,0:T(8,128)(2,1)S(1)}, u32[]{:S(2)}, u32[]{:S(2)}) async-start(bf16[128,80,128]{2,1,0:T(8,128)(2,1)} %shard_map.59), calls=%async_computation.1 | async-start | bytes 5242880 | tf_op jit(solution)/shard_map/all_to_all | solution.py:355
  70.6 41.1 %all-to-all-start = ((bf16[128,80,128]{2,1,0:T(8,128)(2,1)}), bf16[128,80,128]{2,1,0:T(8,128)(2,1)}, u32[]{:S(2)}, u32[]{:S(2)}) async-start(bf16[128,80,128]{2,1,0:T(8,128)(2,1)} %shard_map.60), calls=%async_computation | async-start | bytes 5242880 | tf_op jit(solution)/shard_map/all_to_all | solution.py:355
  76.5 1.7 %copy-start = (bf16[2,2,1024,384]{3,2,1,0:T(8,128)(2,1)}, bf16[2,2,1024,384]{3,2,1,0:T(8,128)(2,1)S(1)}, u32[]{:S(2)}) copy-start(bf16[2,2,1024,384]{3,2,1,0:T(8,128)(2,1)S(1)} %get-tuple-element.9.left_hbm) | copy-start | bytes 9437188
  78.1 1.2 copy-start.1

commit v5 on v4

--- a/solution.py
+++ b/solution.py
@@ -81,7 +81,7 @@
     def inputs(start, count):
         return [s for s in range(start - FILTER_TAPS + 1, start + count) if 0 <= s < FRAMES]
 
-    def filter_antenna(start, count, group, k8):
+    def filter_antenna(start, count, place, group, k8):
         a = group * 8 + k8
         frames = {
             s: x_v[a, slot[s // PIECE] * PIECE + s % PIECE].astype(jnp.float32)
@@ -97,15 +97,16 @@
                     total = term if total is None else total + term
             if total is None:
                 total = jnp.zeros((16, 128), jnp.float32)
-            z[0, q, rows, :] = total[:8] + total[8:]
-            z[1, q, rows, :] = total[:8] - total[8:]
-
-    def transform(count, top, odd):
+            z[0, place + q, rows, :] = total[:8] + total[8:]
+            z[1, place + q, rows, :] = total[:8] - total[8:]
+
+    def transform(count, place, odd):
+        top = 4 * place
         highs, lows = [], []
         for row in range(8):
             piece = jnp.concatenate(
                 [
-                    z[odd, e].reshape(TILE_ANTENNAS // 8, 8, 8, 128)[:, row].reshape(TILE_ANTENNAS, 128)
+                    z[odd, place + e].reshape(TILE_ANTENNAS // 8, 8, 8, 128)[:, row].reshape(TILE_ANTENNAS, 128)
                     for e in range(count)
                 ],
                 axis=0,
@@ -122,23 +123,23 @@
         step = 1024 if count == 8 else 4
         for part in range(2):
             for e in range(count):
-                spectra[pl.ds(step * part + e, DEVICES, stride=8), :] = found[
+                spectra[odd, pl.ds(step * part + e, DEVICES, stride=8), :] = found[
                     128 * part : 128 * part + 128, 128 * e : 128 * e + 128
                 ]
         for n in range(count // 4):
-            rows = spectra[1024 * n : 1024 * (n + 1), :].reshape(DEVICES, 8, 128)
-            place = top + 2 * count * odd + 8 * n
-            out_v[:, place : place + 8, :] = rows.astype(jnp.bfloat16)
+            rows = spectra[odd, 1024 * n : 1024 * (n + 1), :].reshape(DEVICES, 8, 128)
+            row = top + 2 * count * odd + 8 * n
+            out_v[:, row : row + 8, :] = rows.astype(jnp.bfloat16)
 
     waited = 0
-    top = 0
+    place = 0
     leaving = []
     for u, (start, count) in enumerate(units):
         last = max(slot[s // PIECE] for s in inputs(start, count))
 
-        def filter_step(group, _, start=start, count=count):
+        def filter_step(group, _, start=start, count=count, place=place):
             for k8 in range(8):
-                filter_antenna(start, count, group, k8)
+                filter_antenna(start, count, place, group, k8)
             return 0
 
         def filter_share(share, _, last=last, waited=waited, filter_step=filter_step):
@@ -152,16 +153,18 @@
             waited = last + 1
         else:
             lax.fori_loop(0, TILE_ANTENNAS // 8, filter_step, 0)
-        if u == 0:
-            for copy in tables:
-                copy.wait()
+        place += count
+    for copy in tables:
+        copy.wait()
+    place = 0
+    for u, (start, count) in enumerate(units):
         for odd in range(2):
-            transform(count, top, odd)
-        rows = pl.ds(top, 4 * count)
+            transform(count, place, odd)
+        rows = pl.ds(4 * place, 4 * count)
         copy = pltpu.make_async_copy(out_v.at[:, rows], out_hbm.at[:, rows], out_sems.at[u])
         copy.start()
         leaving.append(copy)
-        top += 4 * count
+        place += count
     for copy in leaving:
         copy.wait()
 
@@ -185,8 +188,8 @@
             pltpu.VMEM((FILTER_TAPS, 16, 128), jnp.float32),
             table,
             table,
-            pltpu.VMEM((2, 8, 1024, 128), jnp.float32),
-            pltpu.VMEM((2048, 128), jnp.float32),
+            pltpu.VMEM((2, shape[1] // 4, 1024, 128), jnp.float32),
+            pltpu.VMEM((2, 2048, 128), jnp.float32),
             pltpu.VMEM(shape, jnp.bfloat16),
             pltpu.SemaphoreType.DMA((len(order), SHARES)),
             pltpu.SemaphoreType.DMA((2,)),

time: 122 us -> 121 us (level)
  Pallas kernels: 61.1 us -> 58.7 us
    pallas_call x2, Pallas kernels: 50.1 us -> 47.8 us  [filterbank(): pl.pallas_call(functools.partial(filterbank_kernel, units, tuple(order)),...]
  transfers between devices with their start and end apart: 2 -> 2, of which waited for: 2 -> 2; matrix products, arithmetic and copies ran while one was open for 0% -> 0% of each run, Pallas kernels for 24% -> 23%
where the time goes in v5:
time: 121 us
  Pallas kernels  58.7 us (49%)
  waiting for transfers between devices  41.8 us (35%)
  starting transfers between devices  16.6 us (14%)
  local copies, waits for them, and re-layouts  2.82 us (2%)
    pallas_call x2, Pallas kernels, filterbank(): pl.pallas_call(functools.partial(filterbank_kernel, units, tuple(order)),...  47.8 us
    all_to_all x2, waiting for transfers between devices, exchange(): lax.all_to_all(departing, AXES, split_axis=0, concat_axis=0, tiled=True)  41.8 us
    all_to_all x2, starting transfers between devices, exchange(): lax.all_to_all(departing, AXES, split_axis=0, concat_axis=0, tiled=True)  16.6 us
    pallas_call x1, Pallas kernels, correlate(): pl.pallas_call(correlate_kernel, out_shape=(out, out), in_specs=[anywhere...  10.2 us
    unnamed x4, local copies, waits for them, and re-layouts  2.82 us
  transfers between devices with their start and end apart: 2, of which 2 were waited for; matrix products, arithmetic and copies ran while one was open for 0% of the time, Pallas kernels for 23%

profile of v5, /device:TPU:1, one launch (start us, length us, event | category | flops | bytes accessed | tf_op | source)
XLA Modules:
  0.0 120.8 jit_solution(2826304815011232653)
XLA Ops:
  0.6 20.9 %shard_map.59 = bf16[128,80,128]{2,1,0:T(8,128)(2,1)} custom-call(bf16[128,32,16,128]{3,2,1,0:T(8,128)(2,1)} %bitcast.8, f32[8,1024]{1,0:T(8,128)} %taps_ref.2, bf16[2,1024,256]{2,1,0:T(8,128)(2,1)} %constant.4.clone.high_hbm, bf16[2,1024,256]{2,1,0:T(8,128)(2,1)} %constant.5.clone.low_hbm), custom_call_target="tpu_custom_call" | custom-call | flops 30000001024 | bytes 20971520 | tf_op jit(solution)/shard_map/pallas_call | solution.py:181
  21.5 11.5 %all-to-all-start.1 = ((bf16[128,80,128]{2,1,0:T(8,128)(2,1)}), bf16[128,80,128]{2,1,0:T(8,128)(2,1)S(1)}, u32[]{:S(2)}, u32[]{:S(2)}) async-start(bf16[128,80,128]{2,1,0:T(8,128)(2,1)} %shard_map.59), calls=%async_computation.1 | async-start | bytes 5242880 | tf_op jit(solution)/shard_map/all_to_all | solution.py:358
  33.0 26.9 %shard_map.60 = bf16[128,80,128]{2,1,0:T(8,128)(2,1)} custom-call(bf16[128,32,16,128]{3,2,1,0:T(8,128)(2,1)} %bitcast.9, f32[8,1024]{1,0:T(8,128)} %taps_ref.2, bf16[2,1024,256]{2,1,0:T(8,128)(2,1)} %constant.4.clone.high_hbm, bf16[2,1024,256]{2,1,0:T(8,128)(2,1)} %constant.5.clone.low_hbm), custom_call_target="tpu_custom_call" | custom-call | flops 30000001024 | bytes 20971520 | tf_op jit(solution)/shard_map/pallas_call | solution.py:181
  59.9 9.3 %all-to-all-done.1 = bf16[128,80,128]{2,1,0:T(8,128)(2,1)S(1)} async-done(((bf16[128,80,128]{2,1,0:T(8,128)(2,1)}), bf16[128,80,128]{2,1,0:T(8,128)(2,1)S(1)}, u32[]{:S(2)}, u32[]{:S(2)}) %all-to-all-start.1) | async-done | bytes 2621472 | tf_op jit(solution)/shard_map/all_to_all | solution.py:358
  69.3 5.1 %all-to-all-start = ((bf16[128,80,128]{2,1,0:T(8,128)(2,1)}), bf16[128,80,128]{2,1,0:T(8,128)(2,1)}, u32[]{:S(2)}, u32[]{:S(2)}) async-start(bf16[128,80,128]{2,1,0:T(8,128)(2,1)} %shard_map.60), calls=%async_computation | async-start | bytes 5242880 | tf_op jit(solution)/shard_map/all_to_all | solution.py:358
  74.3 0.8 shard_map.61
  75.1 0.0 copy-start
  75.1 1.6 %copy-done = bf16[2,2,1024,384]{3,2,1,0:T(8,128)(2,1)} copy-done((bf16[2,2,1024,384]{3,2,1,0:T(8,128)(2,1)}, bf16[2,2,1024,384]{3,2,1,0:T(8,128)(2,1)S(1)}, u32[]{:S(2)}) %copy-start) | copy-done | bytes 3145752
  76.8 0.0 copy-start.1
  76.8 1.2 copy-done.1
  77.9 32.4 %all-to-all-done = bf16[128,80,128]{2,1,0:T(8,128)(2,1)} async-done(((bf16[128,80,128]{2,1,0:T(8,128)(2,1)}), bf16[128,80,128]{2,1,0:T(8,128)(2,1)}, u32[]{:S(2)}, u32[]{:S(2)}) %all-to-all-start) | async-done | bytes 2621472 | tf_op jit(solution)/shard_map/all_to_all | solution.py:358
  110.4 10.2 %shard_map.62 = (f32[2,36,128,128]{3,2,1,0:T(8,128)}, f32[2,36,128,128]{3,2,1,0:T(8,128)}) custom-call(bf16[64,2,80,128]{3,2,1,0:T(8,128)(2,1)} %bitcast.5.in_hbm, bf16[2,384,1024]{2,1,0:T(8,128)(2,1)} %copy-done.1, bf16[2,2,1024,384]{3,2,1,0:T(8,128)(2,1)} %copy-done), custom_call_target="tpu_custom_call" | custom-call | flops 5000000000 | bytes 12582912 | tf_op jit(solution)/shard_map/pallas_call | solution.py:338
Async XLA Ops:
  21.5 47.8 %all-to-all-start.1 = ((bf16[128,80,128]{2,1,0:T(8,128)(2,1)}), bf16[128,80,128]{2,1,0:T(8,128)(2,1)S(1)}, u32[]{:S(2)}, u32[]{:S(2)}) async-start(bf16[128,80,128]{2,1,0:T(8,128)(2,1)} %shard_map.59), calls=%async_computation.1 | async-start | bytes 5242880 | tf_op jit(solution)/shard_map/all_to_all | solution.py:358
  69.3 41.1 %all-to-all-start = ((bf16[128,80,128]{2,1,0:T(8,128)(2,1)}), bf16[128,80,128]{2,1,0:T(8,128)(2,1)}, u32[]{:S(2)}, u32[]{:S(2)}) async-start(bf16[128,80,128]{2,1,0:T(8,128)(2,1)} %shard_map.60), calls=%async_computation | async-start | bytes 5242880 | tf_op jit(solution)/shard_map/all_to_all | solution.py:358
  75.1 1.7 %copy-start = (bf16[2,2,1024,384]{3,2,1,0:T(8,128)(2,1)}, bf16[2,2,1024,384]{3,2,1,0:T(8,128)(2,1)S(1)}, u32[]{:S(2)}) copy-start(bf16[2,2,1024,384]{3,2,1,0:T(8,128)(2,1)S(1)} %get-tuple-element.9.left_hbm) | copy-start | bytes 9437188
  76.8 1.2 copy-start.1

commit v6 on v5

--- a/solution.py
+++ b/solution.py
@@ -96,18 +96,19 @@
                     term = taps_rows[k] * frames[s]
                     total = term if total is None else total + term
             if total is None:
-                total = jnp.zeros((16, 128), jnp.float32)
+                continue
             z[0, place + q, rows, :] = total[:8] + total[8:]
             z[1, place + q, rows, :] = total[:8] - total[8:]
 
-    def transform(count, place, odd):
+    def transform(start, count, place, odd):
         top = 4 * place
+        live = sum(1 for e in range(count) if inputs(start + e, 1))
         highs, lows = [], []
         for row in range(8):
             piece = jnp.concatenate(
                 [
                     z[odd, place + e].reshape(TILE_ANTENNAS // 8, 8, 8, 128)[:, row].reshape(TILE_ANTENNAS, 128)
-                    for e in range(count)
+                    for e in range(live)
                 ],
                 axis=0,
             )
@@ -116,16 +117,18 @@
             lows.append((piece - high.astype(jnp.float32)).astype(jnp.bfloat16))
         high = jnp.concatenate(highs, axis=1)
         low = jnp.concatenate(lows, axis=1)
-        size = count * TILE_ANTENNAS
+        size = live * TILE_ANTENNAS
         dot = functools.partial(jnp.dot, preferred_element_type=jnp.float32)
         both = dot(jnp.concatenate([high, low], axis=0), high_ref[odd])
         found = (both[:size] + both[size:] + dot(high, low_ref[odd])).T
         step = 1024 if count == 8 else 4
         for part in range(2):
             for e in range(count):
-                spectra[odd, pl.ds(step * part + e, DEVICES, stride=8), :] = found[
-                    128 * part : 128 * part + 128, 128 * e : 128 * e + 128
-                ]
+                rows = pl.ds(step * part + e, DEVICES, stride=8)
+                if e < live:
+                    spectra[odd, rows, :] = found[128 * part : 128 * part + 128, 128 * e : 128 * e + 128]
+                else:
+                    spectra[odd, rows, :] = jnp.zeros((DEVICES, 128), jnp.float32)
         for n in range(count // 4):
             rows = spectra[odd, 1024 * n : 1024 * (n + 1), :].reshape(DEVICES, 8, 128)
             row = top + 2 * count * odd + 8 * n
@@ -159,7 +162,7 @@
     place = 0
     for u, (start, count) in enumerate(units):
         for odd in range(2):
-            transform(count, place, odd)
+            transform(start, count, place, odd)
         rows = pl.ds(4 * place, 4 * count)
         copy = pltpu.make_async_copy(out_v.at[:, rows], out_hbm.at[:, rows], out_sems.at[u])
         copy.start()

time: 121 us -> 121 us (level)
  no operation moved by 1% of the time
where the time goes in v6:
time: 121 us; the launch traced here: 120 us
  Pallas kernels  58.2 us (48%)
  waiting for transfers between devices  41.8 us (35%)
  starting transfers between devices  16.6 us (14%)
  local copies, waits for them, and re-layouts  2.82 us (2%)
    pallas_call x2, Pallas kernels, filterbank(): pl.pallas_call(functools.partial(filterbank_kernel, units, tuple(order)),...  47.3 us
    all_to_all x2, waiting for transfers between devices, exchange(): lax.all_to_all(departing, AXES, split_axis=0, concat_axis=0, tiled=True)  41.8 us
    all_to_all x2, starting transfers between devices, exchange(): lax.all_to_all(departing, AXES, split_axis=0, concat_axis=0, tiled=True)  16.6 us
    pallas_call x1, Pallas kernels, correlate(): pl.pallas_call(correlate_kernel, out_shape=(out, out), in_specs=[anywhere...  10.2 us
    unnamed x4, local copies, waits for them, and re-layouts  2.82 us
  transfers between devices with their start and end apart: 2, of which 2 were waited for; matrix products, arithmetic and copies ran while one was open for 0% of the time, Pallas kernels for 23%

profile of v6, /device:TPU:1, one launch (start us, length us, event | category | flops | bytes accessed | tf_op | source)
XLA Modules:
  0.0 120.2 jit_solution(16263682972063677302)
XLA Ops:
  0.6 20.4 %shard_map.59 = bf16[128,80,128]{2,1,0:T(8,128)(2,1)} custom-call(bf16[128,32,16,128]{3,2,1,0:T(8,128)(2,1)} %bitcast.8, f32[8,1024]{1,0:T(8,128)} %taps_ref.2, bf16[2,1024,256]{2,1,0:T(8,128)(2,1)} %constant.4.clone.high_hbm, bf16[2,1024,256]{2,1,0:T(8,128)(2,1)} %constant.5.clone.low_hbm), custom_call_target="tpu_custom_call" | custom-call | flops 30000001024 | bytes 20971520 | tf_op jit(solution)/shard_map/pallas_call | solution.py:184
  21.0 11.5 %all-to-all-start.1 = ((bf16[128,80,128]{2,1,0:T(8,128)(2,1)}), bf16[128,80,128]{2,1,0:T(8,128)(2,1)S(1)}, u32[]{:S(2)}, u32[]{:S(2)}) async-start(bf16[128,80,128]{2,1,0:T(8,128)(2,1)} %shard_map.59), calls=%async_computation.1 | async-start | bytes 5242880 | tf_op jit(solution)/shard_map/all_to_all | solution.py:361
  32.5 26.9 %shard_map.60 = bf16[128,80,128]{2,1,0:T(8,128)(2,1)} custom-call(bf16[128,32,16,128]{3,2,1,0:T(8,128)(2,1)} %bitcast.9, f32[8,1024]{1,0:T(8,128)} %taps_ref.2, bf16[2,1024,256]{2,1,0:T(8,128)(2,1)} %constant.4.clone.high_hbm, bf16[2,1024,256]{2,1,0:T(8,128)(2,1)} %constant.5.clone.low_hbm), custom_call_target="tpu_custom_call" | custom-call | flops 30000001024 | bytes 20971520 | tf_op jit(solution)/shard_map/pallas_call | solution.py:184
  59.4 9.3 %all-to-all-done.1 = bf16[128,80,128]{2,1,0:T(8,128)(2,1)S(1)} async-done(((bf16[128,80,128]{2,1,0:T(8,128)(2,1)}), bf16[128,80,128]{2,1,0:T(8,128)(2,1)S(1)}, u32[]{:S(2)}, u32[]{:S(2)}) %all-to-all-start.1) | async-done | bytes 2621472 | tf_op jit(solution)/shard_map/all_to_all | solution.py:361
  68.7 5.1 %all-to-all-start = ((bf16[128,80,128]{2,1,0:T(8,128)(2,1)}), bf16[128,80,128]{2,1,0:T(8,128)(2,1)}, u32[]{:S(2)}, u32[]{:S(2)}) async-start(bf16[128,80,128]{2,1,0:T(8,128)(2,1)} %shard_map.60), calls=%async_computation | async-start | bytes 5242880 | tf_op jit(solution)/shard_map/all_to_all | solution.py:361
  73.8 0.8 shard_map.61
  74.6 0.0 copy-start
  74.6 1.6 %copy-done = bf16[2,2,1024,384]{3,2,1,0:T(8,128)(2,1)} copy-done((bf16[2,2,1024,384]{3,2,1,0:T(8,128)(2,1)}, bf16[2,2,1024,384]{3,2,1,0:T(8,128)(2,1)S(1)}, u32[]{:S(2)}) %copy-start) | copy-done | bytes 3145752
  76.3 0.0 copy-start.1
  76.3 1.2 copy-done.1
  77.4 32.4 %all-to-all-done = bf16[128,80,128]{2,1,0:T(8,128)(2,1)} async-done(((bf16[128,80,128]{2,1,0:T(8,128)(2,1)}), bf16[128,80,128]{2,1,0:T(8,128)(2,1)}, u32[]{:S(2)}, u32[]{:S(2)}) %all-to-all-start) | async-done | bytes 2621472 | tf_op jit(solution)/shard_map/all_to_all | solution.py:361
  109.9 10.2 %shard_map.62 = (f32[2,36,128,128]{3,2,1,0:T(8,128)}, f32[2,36,128,128]{3,2,1,0:T(8,128)}) custom-call(bf16[64,2,80,128]{3,2,1,0:T(8,128)(2,1)} %bitcast.5.in_hbm, bf16[2,384,1024]{2,1,0:T(8,128)(2,1)} %copy-done.1, bf16[2,2,1024,384]{3,2,1,0:T(8,128)(2,1)} %copy-done), custom_call_target="tpu_custom_call" | custom-call | flops 5000000000 | bytes 12582912 | tf_op jit(solution)/shard_map/pallas_call | solution.py:341
Async XLA Ops:
  21.0 47.8 %all-to-all-start.1 = ((bf16[128,80,128]{2,1,0:T(8,128)(2,1)}), bf16[128,80,128]{2,1,0:T(8,128)(2,1)S(1)}, u32[]{:S(2)}, u32[]{:S(2)}) async-start(bf16[128,80,128]{2,1,0:T(8,128)(2,1)} %shard_map.59), calls=%async_computation.1 | async-start | bytes 5242880 | tf_op jit(solution)/shard_map/all_to_all | solution.py:361
  68.7 41.1 %all-to-all-start = ((bf16[128,80,128]{2,1,0:T(8,128)(2,1)}), bf16[128,80,128]{2,1,0:T(8,128)(2,1)}, u32[]{:S(2)}, u32[]{:S(2)}) async-start(bf16[128,80,128]{2,1,0:T(8,128)(2,1)} %shard_map.60), calls=%async_computation | async-start | bytes 5242880 | tf_op jit(solution)/shard_map/all_to_all | solution.py:361
  74.6 1.7 %copy-start = (bf16[2,2,1024,384]{3,2,1,0:T(8,128)(2,1)}, bf16[2,2,1024,384]{3,2,1,0:T(8,128)(2,1)S(1)}, u32[]{:S(2)}) copy-start(bf16[2,2,1024,384]{3,2,1,0:T(8,128)(2,1)S(1)} %get-tuple-element.9.left_hbm) | copy-start | bytes 9437188
  76.3 1.2 copy-start.1

commit v7 on v6

--- a/solution.py
+++ b/solution.py
@@ -273,7 +273,10 @@
         old = pl.ds(0, OLD_DEPTH)
         return (
             pltpu.make_async_copy(y_hbm.at[ch], y.at[ch, old], old_sems.at[ch, 0]),
-            pltpu.make_async_copy(left_hbm.at[ch], left.at[ch, :, :, old], old_sems.at[ch, 1]),
+            pltpu.make_async_copy(left_hbm.at[ch, 0], left.at[ch, 0, :, old], old_sems.at[ch, 1]),
+            pltpu.make_async_copy(
+                left_hbm.at[ch, 1, :, pl.ds(256, 128)], left.at[ch, 1, :, pl.ds(256, 128)], old_sems.at[ch, 2]
+            ),
         )
 
     for ch in range(DEVICE_CHANNELS):
@@ -328,6 +331,8 @@
         prepare(ch)
         for copy in arriving_old(ch):
             copy.wait()
+        left[ch, 1, :, 0:128] = left[ch, 0, :, 128:256]
+        left[ch, 1, :, 128:256] = -left[ch, 0, :, 0:128]
         multiply(ch)
     for ch in range(DEVICE_CHANNELS):
         for pair in range(ANTENNA_BLOCKS // 2):
@@ -349,7 +354,7 @@
             pltpu.VMEM((DEVICE_CHANNELS, 2, ANTENNA_COUNT, DEPTH), jnp.bfloat16),
             pltpu.VMEM((DEVICE_CHANNELS, 2, PAIRS, 128, 128), jnp.float32),
             pltpu.SemaphoreType.DMA((5,)),
-            pltpu.SemaphoreType.DMA((DEVICE_CHANNELS, 2)),
+            pltpu.SemaphoreType.DMA((DEVICE_CHANNELS, 3)),
             pltpu.SemaphoreType.DMA((DEVICE_CHANNELS, ANTENNA_BLOCKS // 2, 2)),
         ],
         compiler_params=pltpu.CompilerParams(vmem_limit_bytes=60 * 2**20),

time: 121 us -> 121 us (level)
  no operation moved by 1% of the time
where the time goes in v7:
time: 121 us
  Pallas kernels  58.6 us (48%)
  waiting for transfers between devices  41.8 us (35%)
  starting transfers between devices  16.6 us (14%)
  local copies, waits for them, and re-layouts  2.82 us (2%)
    pallas_call x2, Pallas kernels, filterbank(): pl.pallas_call(functools.partial(filterbank_kernel, units, tuple(order)),...  47.3 us
    all_to_all x2, waiting for transfers between devices, exchange(): lax.all_to_all(departing, AXES, split_axis=0, concat_axis=0, tiled=True)  41.8 us
    all_to_all x2, starting transfers between devices, exchange(): lax.all_to_all(departing, AXES, split_axis=0, concat_axis=0, tiled=True)  16.6 us
    pallas_call x1, Pallas kernels, correlate(): pl.pallas_call(correlate_kernel, out_shape=(out, out), in_specs=[anywhere...  10.5 us
    unnamed x4, local copies, waits for them, and re-layouts  2.82 us
  transfers between devices with their start and end apart: 2, of which 2 were waited for; matrix products, arithmetic and copies ran while one was open for 0% of the time, Pallas kernels for 23%

profile of v7, /device:TPU:1, one launch (start us, length us, event | category | flops | bytes accessed | tf_op | source)
XLA Modules:
  0.0 120.6 jit_solution(15696090133108169591)
XLA Ops:
  0.6 20.4 %shard_map.59 = bf16[128,80,128]{2,1,0:T(8,128)(2,1)} custom-call(bf16[128,32,16,128]{3,2,1,0:T(8,128)(2,1)} %bitcast.8, f32[8,1024]{1,0:T(8,128)} %taps_ref.2, bf16[2,1024,256]{2,1,0:T(8,128)(2,1)} %constant.4.clone.high_hbm, bf16[2,1024,256]{2,1,0:T(8,128)(2,1)} %constant.5.clone.low_hbm), custom_call_target="tpu_custom_call" | custom-call | flops 30000001024 | bytes 20971520 | tf_op jit(solution)/shard_map/pallas_call | solution.py:184
  21.0 11.5 %all-to-all-start.1 = ((bf16[128,80,128]{2,1,0:T(8,128)(2,1)}), bf16[128,80,128]{2,1,0:T(8,128)(2,1)S(1)}, u32[]{:S(2)}, u32[]{:S(2)}) async-start(bf16[128,80,128]{2,1,0:T(8,128)(2,1)} %shard_map.59), calls=%async_computation.1 | async-start | bytes 5242880 | tf_op jit(solution)/shard_map/all_to_all | solution.py:366
  32.5 26.9 %shard_map.60 = bf16[128,80,128]{2,1,0:T(8,128)(2,1)} custom-call(bf16[128,32,16,128]{3,2,1,0:T(8,128)(2,1)} %bitcast.9, f32[8,1024]{1,0:T(8,128)} %taps_ref.2, bf16[2,1024,256]{2,1,0:T(8,128)(2,1)} %constant.4.clone.high_hbm, bf16[2,1024,256]{2,1,0:T(8,128)(2,1)} %constant.5.clone.low_hbm), custom_call_target="tpu_custom_call" | custom-call | flops 30000001024 | bytes 20971520 | tf_op jit(solution)/shard_map/pallas_call | solution.py:184
  59.4 9.3 %all-to-all-done.1 = bf16[128,80,128]{2,1,0:T(8,128)(2,1)S(1)} async-done(((bf16[128,80,128]{2,1,0:T(8,128)(2,1)}), bf16[128,80,128]{2,1,0:T(8,128)(2,1)S(1)}, u32[]{:S(2)}, u32[]{:S(2)}) %all-to-all-start.1) | async-done | bytes 2621472 | tf_op jit(solution)/shard_map/all_to_all | solution.py:366
  68.7 5.1 %all-to-all-start = ((bf16[128,80,128]{2,1,0:T(8,128)(2,1)}), bf16[128,80,128]{2,1,0:T(8,128)(2,1)}, u32[]{:S(2)}, u32[]{:S(2)}) async-start(bf16[128,80,128]{2,1,0:T(8,128)(2,1)} %shard_map.60), calls=%async_computation | async-start | bytes 5242880 | tf_op jit(solution)/shard_map/all_to_all | solution.py:366
  73.8 0.8 shard_map.61
  74.6 0.0 copy-start
  74.6 1.6 %copy-done = bf16[2,2,1024,384]{3,2,1,0:T(8,128)(2,1)} copy-done((bf16[2,2,1024,384]{3,2,1,0:T(8,128)(2,1)}, bf16[2,2,1024,384]{3,2,1,0:T(8,128)(2,1)S(1)}, u32[]{:S(2)}) %copy-start) | copy-done | bytes 3145752
  76.3 0.0 copy-start.1
  76.3 1.2 copy-done.1
  77.4 32.4 %all-to-all-done = bf16[128,80,128]{2,1,0:T(8,128)(2,1)} async-done(((bf16[128,80,128]{2,1,0:T(8,128)(2,1)}), bf16[128,80,128]{2,1,0:T(8,128)(2,1)}, u32[]{:S(2)}, u32[]{:S(2)}) %all-to-all-start) | async-done | bytes 2621472 | tf_op jit(solution)/shard_map/all_to_all | solution.py:366
  109.9 10.5 %shard_map.62 = (f32[2,36,128,128]{3,2,1,0:T(8,128)}, f32[2,36,128,128]{3,2,1,0:T(8,128)}) custom-call(bf16[64,2,80,128]{3,2,1,0:T(8,128)(2,1)} %bitcast.5.in_hbm, bf16[2,384,1024]{2,1,0:T(8,128)(2,1)} %copy-done.1, bf16[2,2,1024,384]{3,2,1,0:T(8,128)(2,1)} %copy-done), custom_call_target="tpu_custom_call" | custom-call | flops 5000000000 | bytes 12582912 | tf_op jit(solution)/shard_map/pallas_call | solution.py:346
Async XLA Ops:
  21.0 47.8 %all-to-all-start.1 = ((bf16[128,80,128]{2,1,0:T(8,128)(2,1)}), bf16[128,80,128]{2,1,0:T(8,128)(2,1)S(1)}, u32[]{:S(2)}, u32[]{:S(2)}) async-start(bf16[128,80,128]{2,1,0:T(8,128)(2,1)} %shard_map.59), calls=%async_computation.1 | async-start | bytes 5242880 | tf_op jit(solution)/shard_map/all_to_all | solution.py:366
  68.7 41.1 %all-to-all-start = ((bf16[128,80,128]{2,1,0:T(8,128)(2,1)}), bf16[128,80,128]{2,1,0:T(8,128)(2,1)}, u32[]{:S(2)}, u32[]{:S(2)}) async-start(bf16[128,80,128]{2,1,0:T(8,128)(2,1)} %shard_map.60), calls=%async_computation | async-start | bytes 5242880 | tf_op jit(solution)/shard_map/all_to_all | solution.py:366
  74.6 1.7 %copy-start = (bf16[2,2,1024,384]{3,2,1,0:T(8,128)(2,1)}, bf16[2,2,1024,384]{3,2,1,0:T(8,128)(2,1)S(1)}, u32[]{:S(2)}) copy-start(bf16[2,2,1024,384]{3,2,1,0:T(8,128)(2,1)S(1)} %get-tuple-element.9.left_hbm) | copy-start | bytes 9437188
  76.3 1.2 copy-start.1
